TPU v7x, 128 devices: a whole 4x4x4 slice. The times are simulated.
128 devices in a mesh: row: 4 (over x_hi, core), col: 32 (over z, y, x_lo).
Axes of the slice: x: 4 (x_hi: 2, x_lo: 2; x = x_hi * 2 + x_lo), y: 4, z: 4, core: 2. Of those that a mesh axis runs over, the one named last changes fastest.
Arguments:
- t_store: bfloat16 [8192, 1024], P(('row', 'col')), may hold values from -24 to 24
- w_panels: bfloat16 [1024, 65536], P('row', 'col'), may hold values from -0.1875 to 0.1875
- block_place: int32 [1024], replicated, may hold values from 0 to 1023, as said below
- occ_energy: float32 [64], replicated, may hold values from -3 to -0.5
- vir_energy: float32 [1024], replicated, may hold values from 0.3 to 4
- vir_order: int32 [1024], replicated, may hold values from 0 to 1023, each once
Outputs:
- updated: float32 [8192, 65536], P('row', 'col')
Inputs may be any that keep to these rules, and one draw needn't show every extreme that they name: block_place is a permutation of the blocks in which slot s and block block_place[s] lie in the same group of 256 consecutive indices.
All inputs are finite; a program needn't handle non-finite values.
Results may differ from a plain program's by a relative error of at most 0.0003.
Values may be sent and summed in bfloat16 or wider, within the bound.
No kernel may reach another device: no remote copies, remote signals or barrier semaphores. Data moves between devices by JAX's collectives and lax.ppermute only.
A program may use at most 128 MiB of HBM per device.

v0:
```python
import jax
import jax.numpy as jnp
from jax import lax
from jax.sharding import PartitionSpec as P

NOCC = 64
NVIR = 1024
BLK = 8


def per_device(t_store, w_panels, block_place, occ_energy, vir_energy, vir_order):
    row_dev = t_store.shape[0] * lax.axis_size("col")
    col_dev = w_panels.shape[1]
    blk_count = row_dev // BLK
    grid_row = lax.axis_index("row")
    grid_col = lax.axis_index("col")
    local_place = (
        lax.dynamic_slice_in_dim(block_place, grid_row * blk_count, blk_count, 0)
        - grid_row * blk_count
    )
    gathered = lax.all_gather(t_store, "col", axis=0, tiled=True)
    blocks = gathered.reshape(blk_count, BLK, gathered.shape[1])
    amplitudes = (
        jnp.zeros_like(blocks).at[local_place].set(blocks).reshape(row_dev, gathered.shape[1])
    )
    cycle_term = jnp.dot(
        amplitudes,
        lax.all_gather(w_panels, "row", axis=0, tiled=True),
        preferred_element_type=jnp.float32,
    )
    indices = jnp.arange(vir_energy.shape[0], dtype=jnp.int32)
    vir_eff = jnp.sum(
        jnp.where(vir_order[:, None] == indices[None, :], vir_energy[None, :], 0.0), axis=1
    )
    occ_rep = jnp.repeat(occ_energy, NVIR)
    vir_rep = jnp.tile(vir_eff, NOCC)
    row_occ = lax.dynamic_slice_in_dim(occ_rep, grid_row * row_dev, row_dev, 0)
    row_vir = lax.dynamic_slice_in_dim(vir_rep, grid_row * row_dev, row_dev, 0)
    col_occ = lax.dynamic_slice_in_dim(occ_rep, grid_col * col_dev, col_dev, 0)
    col_vir = lax.dynamic_slice_in_dim(vir_rep, grid_col * col_dev, col_dev, 0)
    denominator = row_occ[:, None] + col_occ[None, :] - (row_vir[:, None] + col_vir[None, :])
    return cycle_term / denominator


def solution(mesh):
    in_specs = (P(("row", "col"), None), P("row", "col"), P(), P(), P(), P())
    out_specs = P("row", "col")
    return jax.shard_map(
        per_device, mesh=mesh, in_specs=in_specs, out_specs=out_specs, check_vma=False
    )
```

profile of v0, /device:TPU:0, one launch (start us, length us, event | category | flops | bytes accessed | tf_op | source)
XLA Modules:
  0.0 240.0 jit_solution(16874613810231870079)
XLA Ops:
  6.5 0.0 copy-start
  6.5 0.0 all-gather.3.cloned.1.call-start
  6.5 0.7 all-gather.3.cloned.1.call-update
  7.3 0.0 all-gather.5.cloned.1.call-start
  7.3 0.7 all-gather.5.cloned.1.call-update
  8.0 1.4 select_reduce_fusion
  9.5 0.0 copy-done
  9.5 0.1 broadcast_bitcast_fusion.1
  9.6 0.8 compare_select_fusion
  10.4 166.7 %all-gather.3.cloned.1.call-done = bf16[2048,1024]{1,0:T(8,128)(2,1)} async-done(((bf16[64,1024]{1,0:T(8,128)(2,1)}), bf16[2048,1024]{1,0:T(8,128)(2,1)}) %all-gather.3.cloned.1.call-update) | async-done | bytes 4194320 | tf_op jit(solution)/shard_map/all_gather | solution.py:21
  177.1 2.5 %broadcast_in_dim.28 = bf16[256,8,1024]{2,1,0:T(8,128)(2,1)} broadcast(bf16[]{:T(256)} %constant.10.clone.1), dimensions={} | broadcast | bytes 4194306 | tf_op jit(solution)/shard_map/broadcast_in_dim | solution.py:24
  179.6 33.8 %scatter_fusion = bf16[256,8,1024]{2,1,0:T(8,128)(2,1)} fusion(bf16[256,8,1024]{2,1,0:T(8,128)(2,1)} %broadcast_in_dim.28, s32[256]{0:T(256)S(1)} %compare_select_fusion, bf16[256,8,1024]{2,1,0:T(8,128)(2,1)} %bitcast.14), kind=kCustom, calls=%fused_computation | custom fusion | bytes 12583936 | tf_op jit(solution)/shard_map/scatter | solution.py:24
  213.4 4.3 %all-gather.5.cloned.1.call-done = bf16[1024,2048]{1,0:T(8,128)(2,1)} async-done(((bf16[256,2048]{1,0:T(8,128)(2,1)}), bf16[1024,2048]{1,0:T(8,128)(2,1)}) %all-gather.5.cloned.1.call-update) | async-done | bytes 4194320 | tf_op jit(solution)/shard_map/all_gather | solution.py:28
  217.8 15.4 %subtract_divide_fusion = f32[2048,2048]{1,0:T(8,128)} fusion(f32[2048]{0:T(1024)S(1)} %get-tuple-element.9, f32[2048]{0:T(1024)S(1)} %get-tuple-element.10, f32[2048]{0:T(1024)S(1)} %get-tuple-element.6, f32[2048]{0:T(1024)S(1)} %get-tuple-element.5, bf16[1024,2048]{1,0:T(8,128)(2,1)} %all-gather.5.cloned.1.call-done, bf16[256,8,1024]{2,1,0:T(8,128)(2,1)} %scatter_fusion), kind=kOutput, calls=%fused_computation.1 | convolution fusion | flops 8606711808 | bytes 25198592 | tf_op jit(solution)/shard_map/dot_general | solution.py:26
  (4 shorter events, 0.1 us)
Async XLA Ops:
  6.5 2.9 %copy-start = (f32[64]{0:T(128)S(1)}, f32[64]{0:T(128)}, u32[]{:S(2)}) copy-start(f32[64]{0:T(128)} %param.9) | copy-start | bytes 772
  6.5 170.6 %all-gather.3.cloned.1.call-start = ((), (), s32[]{:S(2)}) async-start(), calls=%async_computation | async-start | bytes 4325376 | tf_op jit(solution)/shard_map/all_gather | solution.py:21
  7.3 210.5 %all-gather.5.cloned.1.call-start = ((), (), s32[]{:S(2)}) async-start(), calls=%async_computation.1 | async-start | bytes 5242880 | tf_op jit(solution)/shard_map/all_gather | solution.py:28
Sparse Core Ops, SparseCore 0:
  9.0 168.0 all-gather.2
  178.8 38.9 all-gather.4
where the time goes:
time: 242 us; the launch traced here: 240 us
  waiting for transfers between devices  172 us (71%)
  local copies, waits for them, and re-layouts  36.5 us (15%)
  matrix products  15.4 us (6%)
  between operations  13.5 us (6%)
    all_gather x1, waiting for transfers between devices, per_device(): gathered = lax.all_gather(t_store, 'col', axis=0, tiled=True)  167 us
    scatter x1, local copies, waits for them, and re-layouts, per_device(): jnp.zeros_like(blocks).at[local_place].set(blocks)  33.8 us
    dot_general x1, matrix products, per_device(): jnp.dot(amplitudes, lax.all_gather(w_panels, 'row', axis=0, tiled=True),...  15.4 us
  transfers between devices with their start and end apart: 2, of which 2 were waited for; matrix products, arithmetic and copies ran while one was open for 16% of the time, Pallas kernels for 0%

commit v1 on v0

v1 whole, which is shorter than its diff:
```python
import functools

import jax
import jax.numpy as jnp
import numpy as np
from jax import lax
from jax.experimental import pallas as pl
from jax.experimental.pallas import tpu as pltpu
from jax.sharding import PartitionSpec as P

NVIR = 1024
BLK = 8
RING = 4
PIECE = 256
TILE = 256


def move(target):
    pairs = []
    for src in range(128):
        row, col = divmod(src, 32)
        place = (row // 2) * 2 + col % 2, col // 2 % RING, col // 8, row % 2
        x, y, z, core = target(*place)
        x, y, z = x % RING, y % RING, z % RING
        pairs.append((src, (x // 2 * 2 + core) * 32 + z * 8 + y * 2 + x % 2))
    return pairs


def along_first(step):
    return move(lambda x, y, z, core: (x, y + step, z, core) if core == 0 else (x, y, z + step, core))


def along_second(step):
    return move(lambda x, y, z, core: (x, y, z + step, core) if core == 0 else (x, y + step, z, core))


ACROSS_LO = move(lambda x, y, z, core: (x ^ 1, y, z, core))
ACROSS_HI = move(lambda x, y, z, core: (x + 2, y, z, core))
OTHER_CORE = move(lambda x, y, z, core: (x, y, z, 1 - core))


def send(value, pairs):
    return lax.ppermute(value, ("row", "col"), pairs)


def multiply(ids, parts, offset, *refs):
    n = len(ids)
    origin, block_place, row_term, col_term = refs[:4]
    pieces = refs[4 : 4 + n]
    panels = refs[4 + n : 4 + n + 4 * parts]
    out, stage, row_part, sem = refs[-4:]
    cols = panels[0].shape[1]
    grid_row = origin[32]

    def place(piece, i):
        slot = origin[ids[piece] * 4 + i // BLK] * BLK + i % BLK
        return block_place[slot] - grid_row * 256

    for piece in range(n):

        def fill(i, carry):
            at = pl.multiple_of(place(piece, i) * BLK, BLK)
            to = pl.multiple_of(piece * PIECE + i * BLK, BLK)
            row_part[pl.ds(to, BLK), :] = row_term[pl.ds(at, BLK), :]
            return carry

        lax.fori_loop(0, PIECE // BLK, fill, 0, unroll=8)
        rows = pl.ds(piece * PIECE, PIECE)
        for part in range(parts):

            def tile(i, carry):
                at = pl.ds(pl.multiple_of(i * TILE, TILE), TILE)
                to = pl.ds(pl.multiple_of(part * cols + i * TILE, TILE), TILE)
                total = None
                for k in range(4):
                    depth = pl.ds(pl.multiple_of((grid_row ^ k) * 256, 256), 256)
                    term = jnp.dot(
                        pieces[piece][:, depth],
                        panels[part * 4 + k][:, at],
                        preferred_element_type=jnp.float32,
                    )
                    total = term if total is None else total + term
                left = row_part[rows, :]
                denominator = jnp.concatenate([left] * (TILE // 128), axis=1) + col_term[:, to]
                inverse = pltpu.reciprocal(denominator, approx=True)
                inverse = inverse * (2.0 - denominator * inverse)
                stage[rows, to] = total * inverse
                return carry

            lax.fori_loop(0, cols // TILE, tile, 0, unroll=4)

        def put(i, carry):
            at = pl.multiple_of(piece * PIECE + i * BLK, BLK)
            to = pl.multiple_of(place(piece, i) * BLK, BLK)
            pltpu.make_async_copy(
                stage.at[pl.ds(at, BLK), :],
                out.at[pl.ds(to, BLK), pl.ds(offset, cols * parts)],
                sem,
            ).start()
            return carry

        lax.fori_loop(0, PIECE // BLK, put, 0, unroll=8)
    pltpu.make_async_copy(
        stage, out.at[pl.ds(0, n * PIECE), pl.ds(offset, cols * parts)], sem
    ).wait()


def contract(result, origin, block_place, row_term, col_term, pieces, panels, offset, shape):
    ids = tuple(pieces)
    parts = len(panels)
    cols = panels[0][0].shape[1] * parts
    operands = [origin, block_place, row_term, col_term[:, offset : offset + cols]]
    operands += list(pieces.values()) + [chunk for part in panels for chunk in part]
    vmem = pl.BlockSpec(memory_space=pltpu.VMEM)
    smem = pl.BlockSpec(memory_space=pltpu.SMEM)
    anywhere = pl.BlockSpec(memory_space=pl.ANY)
    specs = [smem, smem] + [vmem] * (len(operands) - 2)
    alias = {}
    if result is not None:
        alias = {len(operands): 0}
        operands.append(result)
        specs.append(anywhere)
    rows = len(ids) * PIECE
    return pl.pallas_call(
        functools.partial(multiply, ids, parts, offset),
        out_shape=jax.ShapeDtypeStruct(shape, jnp.float32),
        in_specs=specs,
        out_specs=anywhere,
        input_output_aliases=alias,
        scratch_shapes=[
            pltpu.VMEM((rows, cols), jnp.float32),
            pltpu.VMEM((rows, 128), jnp.float32),
            pltpu.SemaphoreType.DMA,
        ],
        compiler_params=pltpu.CompilerParams(vmem_limit_bytes=16 * 2**20),
        cost_estimate=pl.CostEstimate(
            flops=2 * rows * cols * 1024, bytes_accessed=rows * cols * 4, transcendentals=0
        ),
    )(*operands)


NEAR = (0, 3)
FAR = (1, 2)
PIECES = [(NEAR, 0), (FAR, 0), (NEAR, 3), (FAR, 1), (FAR, 3), (NEAR, 1), (NEAR, 2), (FAR, 2)]


def per_device(t_store, w_panels, block_place, occ_energy, vir_energy, vir_order):
    grid_row = lax.axis_index("row")
    grid_col = lax.axis_index("col")
    core = grid_row % 2
    col_dev = w_panels.shape[1]
    row_dev = 2048

    pair = jnp.concatenate([t_store, send(t_store, ACROSS_LO)])
    near = jnp.concatenate([pair, send(pair, along_first(1))])
    far = jnp.concatenate([send(pair, along_first(-1)), send(pair, along_first(2))])
    near_up = send(near, along_second(1))
    far_down = send(far, along_second(-1))
    far_up = send(far, along_second(1))
    near_down = send(near, along_second(-1))
    near_two = send(near_up, along_second(1))
    far_two = send(far_down, along_second(-1))

    half = col_dev // 2
    gate, gated = lax.optimization_barrier((pair, w_panels))
    own = [w_panels[:, :half], w_panels[:, half:]]
    beside = [send(part, OTHER_CORE) for part in own]
    across = [send(gated[:, :half], ACROSS_HI), send(gated[:, half:], ACROSS_HI)]
    aslant = [send(part, OTHER_CORE) for part in across]
    panels = [list(part) for part in zip(own, beside, across, aslant)]

    first = np.array([step for steps, _ in PIECES for step in steps for _ in range(2)], np.int32)
    second = np.array([step for steps, step in PIECES for _ in range(4)], np.int32)
    other = np.array([0, 1] * 16, np.int32)
    y, z, lo = grid_col // 2 % RING, grid_col // 8, grid_col % 2
    at_first = (jnp.where(core == 0, y, z) + first) % RING
    at_second = (jnp.where(core == 0, z, y) + second) % RING
    at_y = jnp.where(core == 0, at_first, at_second)
    at_z = jnp.where(core == 0, at_second, at_first)
    origin = grid_row * 32 + at_z * 8 + at_y * 2 + (lo ^ other)
    origin = jnp.concatenate([origin, grid_row[None]]).astype(jnp.int32)

    indices = jnp.arange(NVIR, dtype=jnp.int32)
    vir_eff = jnp.sum(
        jnp.where(vir_order[:, None] == indices[None, :], vir_energy[None, :], 0.0), axis=1
    )
    row_occ = lax.dynamic_slice_in_dim(occ_energy, grid_row * 2, 2, 0)
    col_occ = lax.dynamic_slice_in_dim(occ_energy, grid_col * 2, 2, 0)
    row_term = jnp.broadcast_to(
        (row_occ[:, None] - vir_eff[None, :]).reshape(row_dev, 1), (row_dev, 128)
    )
    col_term = (col_occ[:, None] - vir_eff[None, :]).reshape(1, col_dev)

    shape = (row_dev, col_dev)
    step = lambda result, pieces, part, offset: contract(
        result, origin, block_place, row_term, col_term, pieces, part, offset, shape
    )
    result = step(None, {0: near, 1: far, 2: near_up}, panels[:1], 0)
    result = step(result, {3: far_down, 4: far_up, 5: near_down}, panels[:1], 0)
    early = {0: near, 1: far, 2: near_up, 3: far_down, 4: far_up, 5: near_down}
    result = step(result, early, panels[1:], half)
    return step(result, {6: near_two, 7: far_two}, panels, 0)


def solution(mesh):
    in_specs = (P(("row", "col"), None), P("row", "col"), P(), P(), P(), P())
    out_specs = P("row", "col")
    return jax.shard_map(
        per_device, mesh=mesh, in_specs=in_specs, out_specs=out_specs, check_vma=False
    )
```

time: 242 us -> 69.8 us (0.29)
  waiting for transfers between devices: 172 us -> 12.9 us
  local copies, waits for them, and re-layouts: 36.5 us -> 4.7 us
  Pallas kernels: 0 us -> 25.3 us
  starting transfers between devices: 0.04 us -> 24.3 us
  matrix products: 15.4 us -> 0 us
  between operations: 13.5 us -> 0.37 us
    all_gather x2 -> x0, waiting for transfers between devices: 171 us -> none  [the longest x1 167 us: per_device(): gathered = lax.all_gather(t_store, 'col', axis=0, tiled=True)]
    scatter x1 -> x0, local copies, waits for them, and re-layouts: 33.8 us -> none  [per_device(): jnp.zeros_like(blocks).at[local_place].set(blocks)]
    pallas_call x0 -> x4, Pallas kernels: none -> 25.3 us  [contract(): pl.pallas_call(functools.partial(multiply, ids, parts, offset), out_shape...]
    ppermute x0 -> x16, starting transfers between devices: none -> 24.3 us  [send(): return lax.ppermute(value, ('row', 'col'), pairs)]
    dot_general x1 -> x0, matrix products: 15.4 us -> none  [per_device(): jnp.dot(amplitudes, lax.all_gather(w_panels, 'row', axis=0, tiled=True),...]
    ppermute x0 -> x16, waiting for transfers between devices: none -> 12.9 us  [send(): return lax.ppermute(value, ('row', 'col'), pairs)]
    slice x0 -> x3, local copies, waits for them, and re-layouts: none -> 2.54 us  [the longest x1 1.27 us: per_device(): own = [w_panels[:, :half], w_panels[:, half:]]]
  transfers between devices with their start and end apart: 2 -> 16, of which waited for: 2 -> 3; matrix products, arithmetic and copies ran while one was open for 16% -> 9% of each run, Pallas kernels for 0% -> 29%
where the time goes in v1:
time: 69.8 us; the launch traced here: 69.1 us
  Pallas kernels  25.3 us (36%)
  starting transfers between devices  24.3 us (35%)
  waiting for transfers between devices  12.9 us (18%)
  local copies, waits for them, and re-layouts  4.7 us (7%)
  other arithmetic  1.53 us (2%)
    pallas_call x4, Pallas kernels, contract(): pl.pallas_call(functools.partial(multiply, ids, parts, offset), out_shape...  25.3 us
    ppermute x16, starting transfers between devices, send(): return lax.ppermute(value, ('row', 'col'), pairs)  24.3 us
    ppermute x16, waiting for transfers between devices, send(): return lax.ppermute(value, ('row', 'col'), pairs)  12.9 us
  transfers between devices with their start and end apart: 16, of which 3 were waited for; matrix products, arithmetic and copies ran while one was open for 9% of the time, Pallas kernels for 29%

profile of v1, /device:TPU:0, one launch (start us, length us, event | category | flops | bytes accessed | tf_op | source)
XLA Modules:
  0.0 69.1 jit_solution(18387153176457407977)
XLA Ops:
  0.0 1.7 %collective-permute-start = (bf16[64,1024]{1,0:T(8,128)(2,1)}, bf16[64,1024]{1,0:T(8,128)(2,1)S(1)}, u32[]{:S(2)}, u32[]{:S(2)}) collective-permute-start(bf16[64,1024]{1,0:T(8,128)(2,1)} %param.9), channel_id=1, source_target_pairs={{0,1},{1,0},{2,3},{3,2},{4,5},{5,4},{6,7},{7,6},{8,9},{9,8},{10,11... | collective-permute-start | bytes 393224 | tf_op jit(solution)/shard_map/ppermute | solution.py:43
  1.7 1.3 %fusion.8 = (bf16[256,1024]{1,0:T(8,128)(2,1)S(1)}, bf16[256,1024]{1,0:T(8,128)(2,1)S(1)}) fusion(bf16[256,2048]{1,0:T(8,128)(2,1)} %param.10), kind=kLoop, calls=%fused_computation.29 | loop fusion | bytes 2097152 | tf_op jit(solution)/shard_map/slice | solution.py:166
  3.0 1.4 %select_reduce_fusion = f32[1024]{0:T(1024)S(1)} fusion(f32[1024]{0:T(1024)} %param.13, s32[1024]{0:T(1024)} %param.14), kind=kLoop, calls=%fused_computation | loop fusion | flops 3144704 | bytes 12288 | tf_op jit(solution)/shard_map/reduce_sum | solution.py:184
  4.4 0.8 %fusion.10 = (f32[2]{0:T(128)S(1)}, f32[2]{0:T(128)S(1)}) fusion(f32[64]{0:T(128)} %param.12, s32[]{:T(128)S(6)} %select_n.74, s32[]{:T(128)S(6)} %select_n.72), kind=kLoop, calls=%fused_computation.31 | loop fusion | bytes 40 | tf_op jit(solution)/shard_map/dynamic_slice | solution.py:188
  5.2 0.9 %constant_dynamic-update-slice_fusion.1 = (bf16[128,1024]{1,0:T(8,128)(2,1)S(1)}, bf16[256,1024]{1,0:T(8,128)(2,1)S(1)}) fusion(bf16[64,1024]{1,0:T(8,128)(2,1)} %param.9), kind=kLoop, calls=%fused_computation.3 | loop fusion | bytes 393216
  6.2 3.1 %collective-permute-start.4 = (bf16[128,1024]{1,0:T(8,128)(2,1)S(1)}, bf16[128,1024]{1,0:T(8,128)(2,1)S(1)}, u32[]{:S(2)}, u32[]{:S(2)}) collective-permute-start(bf16[128,1024]{1,0:T(8,128)(2,1)S(1)} %get-tuple-element.11), channel_id=1, source_target_pairs={{0,6},{1,7},{2,0},{3,1},{4,2},{5,3},{6,4},{7,5},{8,14},{9,15},{10,... | collective-permute-start | bytes 786440 | tf_op jit(solution)/shard_map/ppermute | solution.py:43
  9.3 0.6 collective-permute-start.5
  9.9 1.0 %collective-permute-start.1 = (bf16[128,1024]{1,0:T(8,128)(2,1)S(1)}, bf16[128,1024]{1,0:T(8,128)(2,1)S(1)}, u32[]{:S(2)}, u32[]{:S(2)}) collective-permute-start(bf16[128,1024]{1,0:T(8,128)(2,1)S(1)} %get-tuple-element.11), channel_id=1, source_target_pairs={{0,2},{1,3},{2,4},{3,5},{4,6},{5,7},{6,0},{7,1},{8,10},{9,11},{10,... | collective-permute-start | bytes 786440 | tf_op jit(solution)/shard_map/ppermute | solution.py:43
  10.9 1.3 %fusion.7 = (bf16[256,1024]{1,0:T(8,128)(2,1)S(1)}, bf16[256,1024]{1,0:T(8,128)(2,1)S(1)}) fusion(bf16[256,2048]{1,0:T(8,128)(2,1)} %param.10), kind=kLoop, calls=%fused_computation.28 | loop fusion | bytes 2097152 | tf_op jit(solution)/shard_map/slice | solution.py:168
  12.1 2.8 %collective-permute-start.9 = (bf16[256,1024]{1,0:T(8,128)(2,1)S(1)}, bf16[256,1024]{1,0:T(8,128)(2,1)S(1)}, u32[]{:S(2)}, u32[]{:S(2)}) collective-permute-start(bf16[256,1024]{1,0:T(8,128)(2,1)S(1)} %get-tuple-element.8), channel_id=1, source_target_pairs={{0,64},{1,65},{2,66},{3,67},{4,68},{5,69},{6,70},{7,71},{8,72},{9,... | collective-permute-start | bytes 1572872 | tf_op jit(solution)/shard_map/ppermute | solution.py:43
  14.9 5.0 %collective-permute-done.1 = bf16[128,1024]{1,0:T(8,128)(2,1)S(1)} collective-permute-done((bf16[128,1024]{1,0:T(8,128)(2,1)S(1)}, bf16[128,1024]{1,0:T(8,128)(2,1)S(1)}, u32[]{:S(2)}, u32[]{:S(2)}) %collective-permute-start.1) | collective-permute-done | bytes 262176 | tf_op jit(solution)/shard_map/ppermute | solution.py:43
  19.9 2.7 %collective-permute-start.12 = (bf16[256,1024]{1,0:T(8,128)(2,1)S(1)}, bf16[256,1024]{1,0:T(8,128)(2,1)S(1)}, u32[]{:S(2)}, u32[]{:S(2)}) collective-permute-start(bf16[256,1024]{1,0:T(8,128)(2,1)S(1)} %get-tuple-element.7), channel_id=1, source_target_pairs={{0,64},{1,65},{2,66},{3,67},{4,68},{5,69},{6,70},{7,71},{8,72},{9,... | collective-permute-start | bytes 1572872 | tf_op jit(solution)/shard_map/ppermute | solution.py:43
  22.7 2.0 %collective-permute-start.2 = (bf16[256,1024]{1,0:T(8,128)(2,1)S(1)}, bf16[256,1024]{1,0:T(8,128)(2,1)S(1)}, u32[]{:S(2)}, u32[]{:S(2)}) collective-permute-start(bf16[256,1024]{1,0:T(8,128)(2,1)S(1)} %constant_dynamic-update-slice_fusion.2.refs_4_), channel_id=1, source_target_pairs={{0,8},{1,9},{2,10},{3,11},{4,12},{5,13},{6,14},{7,15},{8,16},{9,17... | collective-permute-start | bytes 1572872 | tf_op jit(solution)/shard_map/ppermute | solution.py:43
  24.8 2.2 %collective-permute-start.6 = (bf16[256,1024]{1,0:T(8,128)(2,1)S(1)}, bf16[256,1024]{1,0:T(8,128)(2,1)S(1)}, u32[]{:S(2)}, u32[]{:S(2)}) collective-permute-start(bf16[256,1024]{1,0:T(8,128)(2,1)S(1)} %constant_dynamic-update-slice_fusion.5.refs_5_), channel_id=1, source_target_pairs={{0,24},{1,25},{2,26},{3,27},{4,28},{5,29},{6,30},{7,31},{8,0},{9,1... | collective-permute-start | bytes 1572872 | tf_op jit(solution)/shard_map/ppermute | solution.py:43
  27.1 1.4 %collective-permute-done.9.refs_9_.refs_8_ = bf16[256,1024]{1,0:T(8,128)(2,1)S(1)} collective-permute-done((bf16[256,1024]{1,0:T(8,128)(2,1)S(1)}, bf16[256,1024]{1,0:T(8,128)(2,1)S(1)}, u32[]{:S(2)}, u32[]{:S(2)}) %collective-permute-start.9) | collective-permute-done | bytes 524320 | tf_op jit(solution)/shard_map/ppermute | solution.py:43
  28.5 4.2 %collective-permute-start.15 = (bf16[256,1024]{1,0:T(8,128)(2,1)S(1)}, bf16[256,1024]{1,0:T(8,128)(2,1)S(1)}, u32[]{:S(2)}, u32[]{:S(2)}) collective-permute-start(bf16[256,1024]{1,0:T(8,128)(2,1)S(1)} %constant_dynamic-update-slice_fusion.2.refs_4_), channel_id=1, source_target_pairs={{0,24},{1,25},{2,26},{3,27},{4,28},{5,29},{6,30},{7,31},{8,0},{9,1... | collective-permute-start | bytes 1572872 | tf_op jit(solution)/shard_map/ppermute | solution.py:43
  32.6 6.5 %collective-permute-done.12.refs_12_ = bf16[256,1024]{1,0:T(8,128)(2,1)S(1)} collective-permute-done((bf16[256,1024]{1,0:T(8,128)(2,1)S(1)}, bf16[256,1024]{1,0:T(8,128)(2,1)S(1)}, u32[]{:S(2)}, u32[]{:S(2)}) %collective-permute-start.12) | collective-permute-done | bytes 524320 | tf_op jit(solution)/shard_map/ppermute | solution.py:43
  39.3 0.5 collective-permute-start.11
  39.9 2.3 %collective-permute-start.7 = (bf16[256,1024]{1,0:T(8,128)(2,1)S(1)}, bf16[256,1024]{1,0:T(8,128)(2,1)S(1)}, u32[]{:S(2)}, u32[]{:S(2)}) collective-permute-start(bf16[256,1024]{1,0:T(8,128)(2,1)S(1)} %collective-permute-done.6.refs_4_.refs_7_), channel_id=1, source_target_pairs={{0,24},{1,25},{2,26},{3,27},{4,28},{5,29},{6,30},{7,31},{8,0},{9,1... | collective-permute-start | bytes 1572872 | tf_op jit(solution)/shard_map/ppermute | solution.py:43
  42.2 1.1 %collective-permute-start.3 = (bf16[256,1024]{1,0:T(8,128)(2,1)S(1)}, bf16[256,1024]{1,0:T(8,128)(2,1)S(1)}, u32[]{:S(2)}, u32[]{:S(2)}) collective-permute-start(bf16[256,1024]{1,0:T(8,128)(2,1)S(1)} %collective-permute-done.2.refs_6_), channel_id=1, source_target_pairs={{0,8},{1,9},{2,10},{3,11},{4,12},{5,13},{6,14},{7,15},{8,16},{9,17... | collective-permute-start | bytes 1572872 | tf_op jit(solution)/shard_map/ppermute | solution.py:43
  43.6 5.2 %shard_map.91.refs_11_ = f32[2048,2048]{1,0:T(8,128)} custom-call(s32[33]{0:T(128)S(1)} %pad_add_fusion.refs_0_, s32[1024]{0:T(1024)S(1)} %copy-done, f32[2048,128]{1,0:T(8,128)S(1)} %broadcast_in_dim.30.refs_2_, f32[1,1024]{1,0:T(1,128)S(1)} %get-tuple-element.15.refs_3_, bf16[256,1024]{1,0:T(8,128)(2,1)S(1)} %constant_dynamic-update-slice_fusion.2.refs_4_, ...), custom_call_target="tpu_custom_call" | custom-call | flops 1610612736 | bytes 3145728 | tf_op jit(solution)/shard_map/pallas_call | solution.py:124
  48.8 5.3 %shard_map.92.refs_14_ = f32[2048,2048]{1,0:T(8,128)} custom-call(s32[33]{0:T(128)S(1)} %pad_add_fusion.refs_0_, s32[1024]{0:T(1024)S(1)} %copy-done, f32[2048,128]{1,0:T(8,128)S(1)} %broadcast_in_dim.30.refs_2_, f32[1,1024]{1,0:T(1,128)S(1)} %get-tuple-element.15.refs_3_, ...), custom_call_target="tpu_custom_call", output_to_operand_aliasing={{}: (11, {})} | custom-call | flops 1610612736 | bytes 3145728 | tf_op jit(solution)/shard_map/pallas_call | solution.py:124
  54.1 9.3 %shard_map.93.refs_14_ = f32[2048,2048]{1,0:T(8,128)} custom-call(s32[33]{0:T(128)S(1)} %pad_add_fusion.refs_0_, s32[1024]{0:T(1024)S(1)} %copy-done, f32[2048,128]{1,0:T(8,128)S(1)} %broadcast_in_dim.30.refs_2_, f32[1,1024]{1,0:T(1,128)S(1)} %get-tuple-element.16.refs_3_, ...), custom_call_target="tpu_custom_call", output_to_operand_aliasing={{}: (14, {})} | custom-call | flops 3221225472 | bytes 6291456 | tf_op jit(solution)/shard_map/pallas_call | solution.py:124
  63.5 5.5 %shard_map.94 = f32[2048,2048]{1,0:T(8,128)} custom-call(s32[33]{0:T(128)S(1)} %pad_add_fusion.refs_0_, s32[1024]{0:T(1024)S(1)} %copy-done, f32[2048,128]{1,0:T(8,128)S(1)} %broadcast_in_dim.30.refs_2_, f32[1,2048]{1,0:T(1,128)S(1)} %bitcast.11, bf16[256,1024]{1,0:T(8,128)(2,1)S(1)} %collective-permute-done.3.refs_4_, ...), custom_call_target="tpu_custom_call", output_to_operand_aliasing={{}: (14, {})} | custom-call | flops 2147483648 | bytes 4194304 | tf_op jit(solution)/shard_map/pallas_call | solution.py:124
  (36 shorter events, 0.9 us)
Async XLA Ops:
  0.0 39.1 %copy-start.1 = (s32[32]{0:T(128)S(1)}, s32[32]{0:T(128)}, u32[]{:S(2)}) copy-start(s32[32]{0:T(128)} %constant.86.clone) | copy-start | bytes 388
  0.0 39.1 %copy-start.2 = (s32[32]{0:T(128)S(1)}, s32[32]{0:T(128)}, u32[]{:S(2)}) copy-start(s32[32]{0:T(128)} %constant.87.clone) | copy-start | bytes 388
  0.0 39.1 %copy-start.3 = (s32[32]{0:T(128)S(1)}, s32[32]{0:T(128)}, u32[]{:S(2)}) copy-start(s32[32]{0:T(128)} %constant.88.clone) | copy-start | bytes 388
  0.0 43.6 %copy-start = (s32[1024]{0:T(1024)S(1)}, s32[1024]{0:T(1024)}, u32[]{:S(2)}) copy-start(s32[1024]{0:T(1024)} %refs_1_.7) | copy-start | bytes 12292
  0.0 6.1 %collective-permute-start = (bf16[64,1024]{1,0:T(8,128)(2,1)}, bf16[64,1024]{1,0:T(8,128)(2,1)S(1)}, u32[]{:S(2)}, u32[]{:S(2)}) collective-permute-start(bf16[64,1024]{1,0:T(8,128)(2,1)} %param.9), channel_id=1, source_target_pairs={{0,1},{1,0},{2,3},{3,2},{4,5},{5,4},{6,7},{7,6},{8,9},{9,8},{10,11... | collective-permute-start | bytes 393224 | tf_op jit(solution)/shard_map/ppermute | solution.py:43
  2.9 24.1 %collective-permute-start.8 = (bf16[256,1024]{1,0:T(8,128)(2,1)S(1)}, bf16[256,1024]{1,0:T(8,128)(2,1)S(1)}, u32[]{:S(2)}, u32[]{:S(2)}) collective-permute-start(bf16[256,1024]{1,0:T(8,128)(2,1)S(1)} %get-tuple-element.10.refs_7_.refs_6_), channel_id=1, source_target_pairs={{0,32},{1,33},{2,34},{3,35},{4,36},{5,37},{6,38},{7,39},{8,40},{9,... | collective-permute-start | bytes 1572872 | tf_op jit(solution)/shard_map/ppermute | solution.py:43
  6.2 16.5 %collective-permute-start.4 = (bf16[128,1024]{1,0:T(8,128)(2,1)S(1)}, bf16[128,1024]{1,0:T(8,128)(2,1)S(1)}, u32[]{:S(2)}, u32[]{:S(2)}) collective-permute-start(bf16[128,1024]{1,0:T(8,128)(2,1)S(1)} %get-tuple-element.11), channel_id=1, source_target_pairs={{0,6},{1,7},{2,0},{3,1},{4,2},{5,3},{6,4},{7,5},{8,14},{9,15},{10,... | collective-permute-start | bytes 786440 | tf_op jit(solution)/shard_map/ppermute | solution.py:43
  9.3 15.5 %collective-permute-start.5 = (bf16[128,1024]{1,0:T(8,128)(2,1)S(1)}, bf16[128,1024]{1,0:T(8,128)(2,1)S(1)}, u32[]{:S(2)}, u32[]{:S(2)}) collective-permute-start(bf16[128,1024]{1,0:T(8,128)(2,1)S(1)} %get-tuple-element.11), channel_id=1, source_target_pairs={{0,4},{1,5},{2,6},{3,7},{4,0},{5,1},{6,2},{7,3},{8,12},{9,13},{10,... | collective-permute-start | bytes 786440 | tf_op jit(solution)/shard_map/ppermute | solution.py:43
  9.9 10.1 %collective-permute-start.1 = (bf16[128,1024]{1,0:T(8,128)(2,1)S(1)}, bf16[128,1024]{1,0:T(8,128)(2,1)S(1)}, u32[]{:S(2)}, u32[]{:S(2)}) collective-permute-start(bf16[128,1024]{1,0:T(8,128)(2,1)S(1)} %get-tuple-element.11), channel_id=1, source_target_pairs={{0,2},{1,3},{2,4},{3,5},{4,6},{5,7},{6,0},{7,1},{8,10},{9,11},{10,... | collective-permute-start | bytes 786440 | tf_op jit(solution)/shard_map/ppermute | solution.py:43
  12.1 16.3 %collective-permute-start.9 = (bf16[256,1024]{1,0:T(8,128)(2,1)S(1)}, bf16[256,1024]{1,0:T(8,128)(2,1)S(1)}, u32[]{:S(2)}, u32[]{:S(2)}) collective-permute-start(bf16[256,1024]{1,0:T(8,128)(2,1)S(1)} %get-tuple-element.8), channel_id=1, source_target_pairs={{0,64},{1,65},{2,66},{3,67},{4,68},{5,69},{6,70},{7,71},{8,72},{9,... | collective-permute-start | bytes 1572872 | tf_op jit(solution)/shard_map/ppermute | solution.py:43
  19.9 19.2 %collective-permute-start.12 = (bf16[256,1024]{1,0:T(8,128)(2,1)S(1)}, bf16[256,1024]{1,0:T(8,128)(2,1)S(1)}, u32[]{:S(2)}, u32[]{:S(2)}) collective-permute-start(bf16[256,1024]{1,0:T(8,128)(2,1)S(1)} %get-tuple-element.7), channel_id=1, source_target_pairs={{0,64},{1,65},{2,66},{3,67},{4,68},{5,69},{6,70},{7,71},{8,72},{9,... | collective-permute-start | bytes 1572872 | tf_op jit(solution)/shard_map/ppermute | solution.py:43
  22.7 16.6 %collective-permute-start.2 = (bf16[256,1024]{1,0:T(8,128)(2,1)S(1)}, bf16[256,1024]{1,0:T(8,128)(2,1)S(1)}, u32[]{:S(2)}, u32[]{:S(2)}) collective-permute-start(bf16[256,1024]{1,0:T(8,128)(2,1)S(1)} %constant_dynamic-update-slice_fusion.2.refs_4_), channel_id=1, source_target_pairs={{0,8},{1,9},{2,10},{3,11},{4,12},{5,13},{6,14},{7,15},{8,16},{9,17... | collective-permute-start | bytes 1572872 | tf_op jit(solution)/shard_map/ppermute | solution.py:43
  24.8 15.0 %collective-permute-start.6 = (bf16[256,1024]{1,0:T(8,128)(2,1)S(1)}, bf16[256,1024]{1,0:T(8,128)(2,1)S(1)}, u32[]{:S(2)}, u32[]{:S(2)}) collective-permute-start(bf16[256,1024]{1,0:T(8,128)(2,1)S(1)} %constant_dynamic-update-slice_fusion.5.refs_5_), channel_id=1, source_target_pairs={{0,24},{1,25},{2,26},{3,27},{4,28},{5,29},{6,30},{7,31},{8,0},{9,1... | collective-permute-start | bytes 1572872 | tf_op jit(solution)/shard_map/ppermute | solution.py:43
  27.0 12.9 %collective-permute-start.14 = (bf16[256,1024]{1,0:T(8,128)(2,1)S(1)}, bf16[256,1024]{1,0:T(8,128)(2,1)S(1)}, u32[]{:S(2)}, u32[]{:S(2)}) collective-permute-start(bf16[256,1024]{1,0:T(8,128)(2,1)S(1)} %constant_dynamic-update-slice_fusion.5.refs_5_), channel_id=1, source_target_pairs={{0,8},{1,9},{2,10},{3,11},{4,12},{5,13},{6,14},{7,15},{8,16},{9,17... | collective-permute-start | bytes 1572872 | tf_op jit(solution)/shard_map/ppermute | solution.py:43
  28.5 20.4 %collective-permute-start.15 = (bf16[256,1024]{1,0:T(8,128)(2,1)S(1)}, bf16[256,1024]{1,0:T(8,128)(2,1)S(1)}, u32[]{:S(2)}, u32[]{:S(2)}) collective-permute-start(bf16[256,1024]{1,0:T(8,128)(2,1)S(1)} %constant_dynamic-update-slice_fusion.2.refs_4_), channel_id=1, source_target_pairs={{0,24},{1,25},{2,26},{3,27},{4,28},{5,29},{6,30},{7,31},{8,0},{9,1... | collective-permute-start | bytes 1572872 | tf_op jit(solution)/shard_map/ppermute | solution.py:43
  39.1 3.0 %collective-permute-start.10 = (bf16[256,1024]{1,0:T(8,128)(2,1)S(1)}, bf16[256,1024]{1,0:T(8,128)(2,1)S(1)}, u32[]{:S(2)}, u32[]{:S(2)}) collective-permute-start(bf16[256,1024]{1,0:T(8,128)(2,1)S(1)} %collective-permute-done.9.refs_9_.refs_8_), channel_id=1, source_target_pairs={{0,32},{1,33},{2,34},{3,35},{4,36},{5,37},{6,38},{7,39},{8,40},{9,... | collective-permute-start | bytes 1572872 | tf_op jit(solution)/shard_map/ppermute | solution.py:43
  39.3 14.8 %collective-permute-start.11 = (bf16[256,1024]{1,0:T(8,128)(2,1)S(1)}, bf16[256,1024]{1,0:T(8,128)(2,1)S(1)}, u32[]{:S(2)}, u32[]{:S(2)}) collective-permute-start(bf16[256,1024]{1,0:T(8,128)(2,1)S(1)} %get-tuple-element.9.refs_10_), channel_id=1, source_target_pairs={{0,32},{1,33},{2,34},{3,35},{4,36},{5,37},{6,38},{7,39},{8,40},{9,... | collective-permute-start | bytes 1572872 | tf_op jit(solution)/shard_map/ppermute | solution.py:43
  39.8 14.3 %collective-permute-start.13 = (bf16[256,1024]{1,0:T(8,128)(2,1)S(1)}, bf16[256,1024]{1,0:T(8,128)(2,1)S(1)}, u32[]{:S(2)}, u32[]{:S(2)}) collective-permute-start(bf16[256,1024]{1,0:T(8,128)(2,1)S(1)} %collective-permute-done.12.refs_12_), channel_id=1, source_target_pairs={{0,32},{1,33},{2,34},{3,35},{4,36},{5,37},{6,38},{7,39},{8,40},{9,... | collective-permute-start | bytes 1572872 | tf_op jit(solution)/shard_map/ppermute | solution.py:43
  39.9 23.6 %collective-permute-start.7 = (bf16[256,1024]{1,0:T(8,128)(2,1)S(1)}, bf16[256,1024]{1,0:T(8,128)(2,1)S(1)}, u32[]{:S(2)}, u32[]{:S(2)}) collective-permute-start(bf16[256,1024]{1,0:T(8,128)(2,1)S(1)} %collective-permute-done.6.refs_4_.refs_7_), channel_id=1, source_target_pairs={{0,24},{1,25},{2,26},{3,27},{4,28},{5,29},{6,30},{7,31},{8,0},{9,1... | collective-permute-start | bytes 1572872 | tf_op jit(solution)/shard_map/ppermute | solution.py:43
  42.2 21.3 %collective-permute-start.3 = (bf16[256,1024]{1,0:T(8,128)(2,1)S(1)}, bf16[256,1024]{1,0:T(8,128)(2,1)S(1)}, u32[]{:S(2)}, u32[]{:S(2)}) collective-permute-start(bf16[256,1024]{1,0:T(8,128)(2,1)S(1)} %collective-permute-done.2.refs_6_), channel_id=1, source_target_pairs={{0,8},{1,9},{2,10},{3,11},{4,12},{5,13},{6,14},{7,15},{8,16},{9,17... | collective-permute-start | bytes 1572872 | tf_op jit(solution)/shard_map/ppermute | solution.py:43

commit v2 on v0

v2 whole, which is shorter than its diff:
```python
import functools

import jax
import jax.numpy as jnp
import numpy as np
from jax import lax
from jax.experimental import pallas as pl
from jax.experimental.pallas import tpu as pltpu
from jax.sharding import PartitionSpec as P

NVIR = 1024
BLK = 8
RING = 4
PIECE = 256
TILE = 256


def move(target):
    pairs = []
    for src in range(128):
        row, col = divmod(src, 32)
        place = (row // 2) * 2 + col % 2, col // 2 % RING, col // 8, row % 2
        x, y, z, core = target(*place)
        x, y, z = x % RING, y % RING, z % RING
        pairs.append((src, (x // 2 * 2 + core) * 32 + z * 8 + y * 2 + x % 2))
    return pairs


def along_first(step):
    return move(lambda x, y, z, core: (x, y + step, z, core) if core == 0 else (x, y, z + step, core))


def along_second(step):
    return move(lambda x, y, z, core: (x, y, z + step, core) if core == 0 else (x, y + step, z, core))


ACROSS_LO = move(lambda x, y, z, core: (x ^ 1, y, z, core))
ACROSS_HI = move(lambda x, y, z, core: (x + 2, y, z, core))
OTHER_CORE = move(lambda x, y, z, core: (x, y, z, 1 - core))


def send(value, pairs):
    return lax.ppermute(value, ("row", "col"), pairs)


def after(value, *others):
    return lax.optimization_barrier((value, *others))[0]


def join_kernel(first, second, out):
    rows = first.shape[0]
    out[:rows, :] = first[...]
    out[rows:, :] = second[...]


def load_kernel(source, out, sem):
    copy = pltpu.make_async_copy(source, out, sem)
    copy.start()
    copy.wait()


def load(source):
    return pl.pallas_call(
        load_kernel,
        out_shape=jax.ShapeDtypeStruct(source.shape, source.dtype),
        in_specs=[pl.BlockSpec(memory_space=pl.ANY)],
        out_specs=pl.BlockSpec(memory_space=pltpu.VMEM),
        scratch_shapes=[pltpu.SemaphoreType.DMA],
        compiler_params=limits(1),
        cost_estimate=cost(0, 2**20),
    )(source)


def join(first, second):
    rows, cols = first.shape
    vmem = pl.BlockSpec(memory_space=pltpu.VMEM)
    return pl.pallas_call(
        join_kernel,
        out_shape=jax.ShapeDtypeStruct((2 * rows, cols), first.dtype),
        in_specs=[vmem, vmem],
        out_specs=vmem,
        compiler_params=limits(4),
        cost_estimate=cost(0, 8 * rows * cols),
    )(first, second)


def arrange(origin, block_place, row_term, row_part, places):
    grid_row = origin[32]

    def block(i, carry):
        place = block_place[origin[i // BLK] * BLK + i % BLK] - grid_row * 256
        places[i] = place
        at, to = pl.multiple_of(place * BLK, BLK), pl.multiple_of(i * BLK, BLK)
        row_part[pl.ds(to, BLK), :] = row_term[pl.ds(at, BLK), :]
        return carry

    lax.fori_loop(0, 256, block, 0, unroll=8)


def begin(pair, origin, *refs):
    first, second, own, beside = refs[:4]
    held, sums = refs[-2:]
    grid_row = origin[32]
    rows = pl.ds(pair * 2 * PIECE, 2 * PIECE)
    held[pl.ds(pair * 2 * PIECE, PIECE), :] = first[...]
    held[pl.ds((pair * 2 + 1) * PIECE, PIECE), :] = second[...]

    def tile(i, carry):
        at = pl.ds(pl.multiple_of(i * TILE, TILE), TILE)
        total = None
        for chunk, panel in enumerate((own, beside)):
            depth = pl.ds(pl.multiple_of((grid_row ^ chunk) * 256, 256), 256)
            left = jnp.concatenate([first[:, depth], second[:, depth]])
            term = jnp.dot(left, panel[:, at], preferred_element_type=jnp.float32)
            total = term if total is None else total + term
        sums[rows, at] = total
        return carry

    lax.fori_loop(0, sums.shape[1] // TILE, tile, 0, unroll=4)


def finish(origin, places, row_part, col_term, held, sums, across, aslant, out, stage, sem):
    cols = col_term.shape[1]
    tiles, blocks = cols // TILE, 2 * PIECE // BLK
    depths = [pl.ds(pl.multiple_of((origin[32] ^ chunk) * 256, 256), 256) for chunk in (2, 3)]

    def gone(slot):
        pltpu.make_async_copy(
            stage.at[slot], out.at[pl.ds(0, 2 * PIECE), :], sem.at[slot]
        ).wait()

    def work(pair, carry):
        slot = pair % 2
        rows = pl.ds(pl.multiple_of(pair * 2 * PIECE, 2 * PIECE), 2 * PIECE)

        @pl.when(pair > 1)
        def _():
            gone(slot)

        def tile(i, carry):
            at = pl.ds(pl.multiple_of(i * TILE, TILE), TILE)
            total = sums[rows, at]
            for depth, panel in zip(depths, (across, aslant)):
                total += jnp.dot(held[rows, depth], panel[:, at], preferred_element_type=jnp.float32)
            left = row_part[rows, :]
            denominator = jnp.concatenate([left] * (TILE // 128), axis=1) + col_term[:, at]
            inverse = pltpu.reciprocal(denominator, approx=True)
            inverse = inverse * (2.0 - denominator * inverse)
            stage[slot, :, at] = total * inverse
            return carry

        lax.fori_loop(0, tiles, tile, 0, unroll=8)

        def put(i, carry):
            at = pl.multiple_of(i * BLK, BLK)
            to = pl.multiple_of(places[pair * blocks + i] * BLK, BLK)
            pltpu.make_async_copy(
                stage.at[slot, pl.ds(at, BLK), :], out.at[pl.ds(to, BLK), :], sem.at[slot]
            ).start()
            return carry

        lax.fori_loop(0, blocks, put, 0, unroll=64)
        return carry

    lax.fori_loop(0, 4, work, 0)
    gone(0)
    gone(1)


VMEM = pl.BlockSpec(memory_space=pltpu.VMEM)
SMEM = pl.BlockSpec(memory_space=pltpu.SMEM)


def limits(mebibytes):
    return pltpu.CompilerParams(vmem_limit_bytes=mebibytes * 2**20)


def cost(flops, moved):
    return pl.CostEstimate(flops=flops, bytes_accessed=moved, transcendentals=0)


def arranged(origin, block_place, row_term):
    return pl.pallas_call(
        arrange,
        out_shape=[
            jax.ShapeDtypeStruct(row_term.shape, jnp.float32),
            jax.ShapeDtypeStruct((256,), jnp.int32),
        ],
        in_specs=[SMEM, SMEM, VMEM],
        out_specs=[VMEM, SMEM],
        compiler_params=limits(4),
        cost_estimate=cost(0, 2**21),
    )(origin, block_place, row_term)


def begun(pair, work, origin, pieces, own, beside, so_far, *awaited):
    cols, depth = own.shape[1], pieces[0].shape[1]
    shapes = [
        jax.ShapeDtypeStruct((8 * PIECE, depth), own.dtype),
        jax.ShapeDtypeStruct((8 * PIECE, cols), jnp.float32),
    ]
    operands = [origin, *pieces, own, beside, *so_far, *awaited]
    return pl.pallas_call(
        functools.partial(begin, pair),
        out_shape=shapes,
        in_specs=[SMEM]
        + [VMEM] * (len(operands) - 1 - len(awaited))
        + [pl.BlockSpec(memory_space=pl.ANY)] * len(awaited),
        out_specs=[VMEM, VMEM],
        input_output_aliases={5: 0, 6: 1} if so_far else {},
        compiler_params=limits(4),
        cost_estimate=cost(work, 2**21),
    )(*operands)


def finished(*operands):
    shape = operands[2].shape[0], operands[3].shape[1]
    return pl.pallas_call(
        finish,
        out_shape=jax.ShapeDtypeStruct(shape, jnp.float32),
        in_specs=[SMEM, SMEM] + [VMEM] * 6,
        out_specs=pl.BlockSpec(memory_space=pl.ANY),
        scratch_shapes=[
            pltpu.VMEM((2, 2 * PIECE, shape[1]), jnp.float32),
            pltpu.SemaphoreType.DMA((2,)),
        ],
        compiler_params=limits(12),
        cost_estimate=cost(1, 2**23),
    )(*operands)


NEAR = (0, 3)
FAR = (1, 2)
PIECES = [(NEAR, 0), (FAR, 0), (NEAR, 3), (FAR, 1), (FAR, 3), (NEAR, 1), (NEAR, 2), (FAR, 2)]


def per_device(t_store, w_panels, block_place, occ_energy, vir_energy, vir_order):
    grid_row = lax.axis_index("row")
    grid_col = lax.axis_index("col")
    core = grid_row % 2
    col_dev = w_panels.shape[1]
    row_dev = 2048

    first = np.array([step for steps, _ in PIECES for step in steps for _ in range(2)], np.int32)
    second = np.array([step for steps, step in PIECES for _ in range(4)], np.int32)
    other = np.array([0, 1] * 16, np.int32)
    y, z, lo = grid_col // 2 % RING, grid_col // 8, grid_col % 2
    at_first = (jnp.where(core == 0, y, z) + first) % RING
    at_second = (jnp.where(core == 0, z, y) + second) % RING
    at_y = jnp.where(core == 0, at_first, at_second)
    at_z = jnp.where(core == 0, at_second, at_first)
    origin = grid_row * 32 + at_z * 8 + at_y * 2 + (lo ^ other)
    origin = jnp.concatenate([origin, grid_row[None]]).astype(jnp.int32)

    indices = jnp.arange(NVIR, dtype=jnp.int32)
    vir_eff = jnp.sum(
        jnp.where(vir_order[:, None] == indices[None, :], vir_energy[None, :], 0.0), axis=1
    )
    row_occ = lax.dynamic_slice_in_dim(occ_energy, grid_row * 2, 2, 0)
    col_occ = lax.dynamic_slice_in_dim(occ_energy, grid_col * 2, 2, 0)
    row_term = jnp.broadcast_to(
        (row_occ[:, None] - vir_eff[None, :]).reshape(row_dev, 1), (row_dev, 128)
    )
    col_term = (col_occ[:, None] - vir_eff[None, :]).reshape(1, col_dev)

    own = load(t_store)
    pair = join(own, send(t_store, ACROSS_LO))
    beside = send(w_panels, OTHER_CORE)
    row_part, places = arranged(origin, block_place, row_term)
    near = join(after(pair, row_part, places, col_term, beside), send(pair, along_first(1)))
    far = join(after(send(pair, along_first(-1)), near), send(pair, along_first(2)))
    near_up = send(near, along_second(1))
    far_down = send(far, along_second(-1))
    far_up = send(far, along_second(1))
    near_down = send(after(near, far), along_second(-1))
    near_two = send(near_up, along_second(1))
    far_two = send(far_down, along_second(-1))

    across = send(after(w_panels, own), ACROSS_HI)
    so_far = begun(0, int(3 * 10**9), origin, (near, far), w_panels, beside, [])
    so_far = begun(1, int(3 * 10**9), origin, (near_up, far_down), w_panels, beside, so_far)
    so_far = begun(2, int(3 * 10**9), origin, (far_up, near_down), w_panels, beside, so_far, across)
    aslant = send(after(across, so_far[1]), OTHER_CORE)
    held, sums = begun(3, 12 * 10**9, origin, (near_two, far_two), w_panels, beside, so_far)
    return finished(origin, places, row_part, col_term, held, sums, across, aslant)


def solution(mesh):
    in_specs = (P(("row", "col"), None), P("row", "col"), P(), P(), P(), P())
    out_specs = P("row", "col")
    return jax.shard_map(
        per_device, mesh=mesh, in_specs=in_specs, out_specs=out_specs, check_vma=False
    )
```

time: 242 us -> 57.1 us (0.24)
  waiting for transfers between devices: 172 us -> 9.04 us
  local copies, waits for them, and re-layouts: 36.5 us -> 2.77 us
  Pallas kernels: 0 us -> 21.8 us
  starting transfers between devices: 0.04 us -> 20.9 us
  matrix products: 15.4 us -> 0 us
  between operations: 13.5 us -> 0.18 us
    all_gather x2 -> x0, waiting for transfers between devices: 171 us -> none  [the longest x1 167 us: per_device(): gathered = lax.all_gather(t_store, 'col', axis=0, tiled=True)]
    scatter x1 -> x0, local copies, waits for them, and re-layouts: 33.8 us -> none  [per_device(): jnp.zeros_like(blocks).at[local_place].set(blocks)]
    pallas_call x0 -> x10, Pallas kernels: none -> 21.8 us  [the longest x1 9.29 us: finished(): pl.pallas_call(finish, out_shape=jax.ShapeDtypeStruct(shape, jnp.float32)...]
    ppermute x0 -> x13, starting transfers between devices: none -> 20.9 us  [send(): return lax.ppermute(value, ('row', 'col'), pairs)]
    dot_general x1 -> x0, matrix products: 15.4 us -> none  [per_device(): jnp.dot(amplitudes, lax.all_gather(w_panels, 'row', axis=0, tiled=True),...]
    ppermute x0 -> x13, waiting for transfers between devices: none -> 9.04 us  [send(): return lax.ppermute(value, ('row', 'col'), pairs)]
  transfers between devices with their start and end apart: 2 -> 13, of which waited for: 2 -> 4; matrix products, arithmetic and copies ran while one was open for 16% -> 6% of each run, Pallas kernels for 0% -> 22%
where the time goes in v2:
time: 57.1 us; the launch traced here: 56.9 us
  Pallas kernels  21.8 us (38%)
  starting transfers between devices  20.9 us (37%)
  waiting for transfers between devices  9.04 us (16%)
  local copies, waits for them, and re-layouts  2.77 us (5%)
  other arithmetic  2.21 us (4%)
    ppermute x13, starting transfers between devices, send(): return lax.ppermute(value, ('row', 'col'), pairs)  20.9 us
    pallas_call x1, Pallas kernels, finished(): pl.pallas_call(finish, out_shape=jax.ShapeDtypeStruct(shape, jnp.float32)...  9.29 us
    ppermute x13, waiting for transfers between devices, send(): return lax.ppermute(value, ('row', 'col'), pairs)  9.04 us
    pallas_call x4, Pallas kernels, begun(): pl.pallas_call(functools.partial(begin, pair), out_shape=shapes, in_specs...  8.83 us
    pallas_call x1, Pallas kernels, arranged(): pl.pallas_call(arrange, out_shape=[jax.ShapeDtypeStruct(row_term.shape, j...  3.39 us
    unnamed x8, local copies, waits for them, and re-layouts  1.64 us
    reduce_sum x1, other arithmetic, per_device(): jnp.sum(jnp.where(vir_order[:, None] == indices[None, :], vir_energy[None...  1.35 us
  transfers between devices with their start and end apart: 13, of which 4 were waited for; matrix products, arithmetic and copies ran while one was open for 6% of the time, Pallas kernels for 22%

profile of v2, /device:TPU:0, one launch (start us, length us, event | category | flops | bytes accessed | tf_op | source)
XLA Modules:
  0.0 56.9 jit_solution(3317104656921141852)
XLA Ops:
  0.0 1.6 %collective-permute-start = (bf16[64,1024]{1,0:T(8,128)(2,1)}, bf16[64,1024]{1,0:T(8,128)(2,1)S(1)}, u32[]{:S(2)}, u32[]{:S(2)}) collective-permute-start(bf16[64,1024]{1,0:T(8,128)(2,1)} %source.1), channel_id=1, source_target_pairs={{0,1},{1,0},{2,3},{3,2},{4,5},{5,4},{6,7},{7,6},{8,9},{9,8},{10,11... | collective-permute-start | bytes 393224 | tf_op jit(solution)/shard_map/ppermute | solution.py:43
  1.7 0.9 %copy-done.1 = bf16[64,1024]{1,0:T(8,128)(2,1)S(1)} copy-done((bf16[64,1024]{1,0:T(8,128)(2,1)S(1)}, bf16[64,1024]{1,0:T(8,128)(2,1)}, u32[]{:S(2)}) %copy-start.1) | copy-done | bytes 131096
  2.7 2.8 %collective-permute-start.11 = (bf16[256,2048]{1,0:T(8,128)(2,1)}, bf16[256,2048]{1,0:T(8,128)(2,1)S(1)}, u32[]{:S(2)}, u32[]{:S(2)}) collective-permute-start(bf16[256,2048]{1,0:T(8,128)(2,1)} %refs_2_.7), channel_id=1, source_target_pairs={{0,64},{1,65},{2,66},{3,67},{4,68},{5,69},{6,70},{7,71},{8,72},{9,... | collective-permute-start | bytes 3145736 | tf_op jit(solution)/shard_map/ppermute | solution.py:43
  5.6 0.8 %fusion.7 = (f32[2]{0:T(128)S(1)}, f32[2]{0:T(128)S(1)}) fusion(f32[64]{0:T(128)} %param.12, s32[]{:T(128)S(6)} %select_n.74, s32[]{:T(128)S(6)} %select_n.72), kind=kLoop, calls=%fused_computation.21 | loop fusion | bytes 40 | tf_op jit(solution)/shard_map/dynamic_slice | solution.py:260
  6.4 1.4 %select_reduce_fusion = f32[1024]{0:T(1024)S(1)} fusion(f32[1024]{0:T(1024)} %param.13, s32[1024]{0:T(1024)} %param.14), kind=kLoop, calls=%fused_computation | loop fusion | flops 3144704 | bytes 12288 | tf_op jit(solution)/shard_map/reduce_sum | solution.py:256
  7.9 1.6 %collective-permute-start.2 = (bf16[128,1024]{1,0:T(8,128)(2,1)S(1)}, bf16[128,1024]{1,0:T(8,128)(2,1)S(1)}, u32[]{:S(2)}, u32[]{:S(2)}) collective-permute-start(bf16[128,1024]{1,0:T(8,128)(2,1)S(1)} %shard_map.93.first), channel_id=1, source_target_pairs={{0,2},{1,3},{2,4},{3,5},{4,6},{5,7},{6,0},{7,1},{8,10},{9,11},{10,... | collective-permute-start | bytes 786440 | tf_op jit(solution)/shard_map/ppermute | solution.py:43
  9.5 1.7 %collective-permute-start.5 = (bf16[128,1024]{1,0:T(8,128)(2,1)S(1)}, bf16[128,1024]{1,0:T(8,128)(2,1)S(1)}, u32[]{:S(2)}, u32[]{:S(2)}) collective-permute-start(bf16[128,1024]{1,0:T(8,128)(2,1)S(1)} %shard_map.93.first), channel_id=1, source_target_pairs={{0,6},{1,7},{2,0},{3,1},{4,2},{5,3},{6,4},{7,5},{8,14},{9,15},{10,... | collective-permute-start | bytes 786440 | tf_op jit(solution)/shard_map/ppermute | solution.py:43
  11.2 2.0 %collective-permute-start.6 = (bf16[128,1024]{1,0:T(8,128)(2,1)S(1)}, bf16[128,1024]{1,0:T(8,128)(2,1)S(1)}, u32[]{:S(2)}, u32[]{:S(2)}) collective-permute-start(bf16[128,1024]{1,0:T(8,128)(2,1)S(1)} %shard_map.93.first), channel_id=1, source_target_pairs={{0,4},{1,5},{2,6},{3,7},{4,0},{5,1},{6,2},{7,3},{8,12},{9,13},{10,... | collective-permute-start | bytes 786440 | tf_op jit(solution)/shard_map/ppermute | solution.py:43
  13.1 0.7 %fusion.6 = s32[32]{0:T(128)S(1)} fusion(s32[32]{0:T(128)} %constant.86.clone, s32[32]{0:T(128)} %constant.87.clone, pred[]{:T(512)S(6)} %eq.26, s32[32]{0:T(128)} %constant.88.clone, s32[]{:T(128)S(6)} %select_n.71, s32[]{:T(128)S(6)} %select_n.67, s32[]{:T(128)S(6)} %select_n.65, s32[]{:T(128)S(6)} %mul.21), kind=kLoop, calls=%fused_computation.19 | loop fusion | flops 1024 | bytes 529 | tf_op jit(solution)/shard_map/add | solution.py:252
  13.9 0.3 broadcast_in_dim.30.row_term
  14.3 0.7 %copy-done.2 = s32[1024]{0:T(1024)S(1)} copy-done((s32[1024]{0:T(1024)S(1)}, s32[1024]{0:T(1024)}, u32[]{:S(2)}) %copy-start.2) | copy-done | bytes 4120
  15.0 3.4 %shard_map.91 = (f32[2048,128]{1,0:T(8,128)S(1)}, s32[256]{0:T(256)S(1)}) custom-call(s32[33]{0:T(128)S(1)} %pad_add_fusion.origin, s32[1024]{0:T(1024)S(1)} %copy-done.2, f32[2048,128]{1,0:T(8,128)S(1)} %broadcast_in_dim.30.row_term), custom_call_target="tpu_custom_call" | custom-call | bytes 2097152 | tf_op jit(solution)/shard_map/pallas_call | solution.py:183
  18.4 1.1 %collective-permute-done.6.second = bf16[128,1024]{1,0:T(8,128)(2,1)S(1)} collective-permute-done((bf16[128,1024]{1,0:T(8,128)(2,1)S(1)}, bf16[128,1024]{1,0:T(8,128)(2,1)S(1)}, u32[]{:S(2)}, u32[]{:S(2)}) %collective-permute-start.6) | collective-permute-done | bytes 262176 | tf_op jit(solution)/shard_map/ppermute | solution.py:43
  19.6 4.1 %collective-permute-start.7 = (bf16[256,1024]{1,0:T(8,128)(2,1)S(1)}, bf16[256,1024]{1,0:T(8,128)(2,1)S(1)}, u32[]{:S(2)}, u32[]{:S(2)}) collective-permute-start(bf16[256,1024]{1,0:T(8,128)(2,1)S(1)} %shard_map.95.refs_1_), channel_id=1, source_target_pairs={{0,24},{1,25},{2,26},{3,27},{4,28},{5,29},{6,30},{7,31},{8,0},{9,1... | collective-permute-start | bytes 1572872 | tf_op jit(solution)/shard_map/ppermute | solution.py:43
  23.7 3.3 %collective-permute-start.10 = (bf16[256,1024]{1,0:T(8,128)(2,1)S(1)}, bf16[256,1024]{1,0:T(8,128)(2,1)S(1)}, u32[]{:S(2)}, u32[]{:S(2)}) collective-permute-start(bf16[256,1024]{1,0:T(8,128)(2,1)S(1)} %shard_map.94.refs_0_), channel_id=1, source_target_pairs={{0,24},{1,25},{2,26},{3,27},{4,28},{5,29},{6,30},{7,31},{8,0},{9,1... | collective-permute-start | bytes 1572872 | tf_op jit(solution)/shard_map/ppermute | solution.py:43
  27.0 2.2 %shard_map.96 = (bf16[2048,1024]{1,0:T(8,128)(2,1)S(1)}, f32[2048,2048]{1,0:T(8,128)S(1)}) custom-call(s32[33]{0:T(128)S(1)} %pad_add_fusion.origin, bf16[256,1024]{1,0:T(8,128)(2,1)S(1)} %shard_map.94.refs_0_, bf16[256,1024]{1,0:T(8,128)(2,1)S(1)} %shard_map.95.refs_1_, bf16[256,2048]{1,0:T(8,128)(2,1)S(1)} %copy-done, ...), custom_call_target="tpu_custom_call" | custom-call | flops 3000000000 | bytes 2097152 | tf_op jit(solution)/shard_map/pallas_call | solution.py:203
  29.2 1.2 %collective-permute-done.7.refs_1_ = bf16[256,1024]{1,0:T(8,128)(2,1)S(1)} collective-permute-done((bf16[256,1024]{1,0:T(8,128)(2,1)S(1)}, bf16[256,1024]{1,0:T(8,128)(2,1)S(1)}, u32[]{:S(2)}, u32[]{:S(2)}) %collective-permute-start.7) | collective-permute-done | bytes 524320 | tf_op jit(solution)/shard_map/ppermute | solution.py:43
  30.4 3.7 %collective-permute-start.8 = (bf16[256,1024]{1,0:T(8,128)(2,1)S(1)}, bf16[256,1024]{1,0:T(8,128)(2,1)S(1)}, u32[]{:S(2)}, u32[]{:S(2)}) collective-permute-start(bf16[256,1024]{1,0:T(8,128)(2,1)S(1)} %collective-permute-done.7.refs_1_), channel_id=1, source_target_pairs={{0,24},{1,25},{2,26},{3,27},{4,28},{5,29},{6,30},{7,31},{8,0},{9,1... | collective-permute-start | bytes 1572872 | tf_op jit(solution)/shard_map/ppermute | solution.py:43
  34.1 2.2 %shard_map.97 = (bf16[2048,1024]{1,0:T(8,128)(2,1)S(1)}, f32[2048,2048]{1,0:T(8,128)S(1)}) custom-call(s32[33]{0:T(128)S(1)} %pad_add_fusion.origin, bf16[256,1024]{1,0:T(8,128)(2,1)S(1)} %collective-permute-done.3.refs_0_, bf16[256,1024]{1,0:T(8,128)(2,1)S(1)} %collective-permute-done.7.refs_1_, ...), custom_call_target="tpu_custom_call", output_to_operand_aliasing={{0}: (5, {}), {1}: (6, {})} | custom-call | flops 3000000000 | bytes 2097152 | tf_op jit(solution)/shard_map/pallas_call | solution.py:203
  36.3 3.4 %collective-permute-done.9.refs_0_ = bf16[256,1024]{1,0:T(8,128)(2,1)S(1)} collective-permute-done((bf16[256,1024]{1,0:T(8,128)(2,1)S(1)}, bf16[256,1024]{1,0:T(8,128)(2,1)S(1)}, u32[]{:S(2)}, u32[]{:S(2)}) %collective-permute-start.9) | collective-permute-done | bytes 524320 | tf_op jit(solution)/shard_map/ppermute | solution.py:43
  39.7 2.2 %shard_map.98 = (bf16[2048,1024]{1,0:T(8,128)(2,1)S(1)}, f32[2048,2048]{1,0:T(8,128)S(1)}) custom-call(s32[33]{0:T(128)S(1)} %pad_add_fusion.origin, bf16[256,1024]{1,0:T(8,128)(2,1)S(1)} %collective-permute-done.9.refs_0_, bf16[256,1024]{1,0:T(8,128)(2,1)S(1)} %collective-permute-done.10.refs_1_, ...), custom_call_target="tpu_custom_call", output_to_operand_aliasing={{0}: (5, {}), {1}: (6, {})} | custom-call | flops 3000000000 | bytes 2097152 | tf_op jit(solution)/shard_map/pallas_call | solution.py:203
  42.0 3.3 %collective-permute-done.4.refs_0_ = bf16[256,1024]{1,0:T(8,128)(2,1)S(1)} collective-permute-done((bf16[256,1024]{1,0:T(8,128)(2,1)S(1)}, bf16[256,1024]{1,0:T(8,128)(2,1)S(1)}, u32[]{:S(2)}, u32[]{:S(2)}) %collective-permute-start.4) | collective-permute-done | bytes 524320 | tf_op jit(solution)/shard_map/ppermute | solution.py:43
  45.3 2.2 %shard_map.99 = (bf16[2048,1024]{1,0:T(8,128)(2,1)S(1)}, f32[2048,2048]{1,0:T(8,128)S(1)}) custom-call(s32[33]{0:T(128)S(1)} %pad_add_fusion.origin, bf16[256,1024]{1,0:T(8,128)(2,1)S(1)} %collective-permute-done.4.refs_0_, bf16[256,1024]{1,0:T(8,128)(2,1)S(1)} %collective-permute-done.8.refs_1_, ...), custom_call_target="tpu_custom_call", output_to_operand_aliasing={{0}: (5, {}), {1}: (6, {})} | custom-call | flops 12000000000 | bytes 2097152 | tf_op jit(solution)/shard_map/pallas_call | solution.py:203
  47.6 9.3 %shard_map.100 = f32[2048,2048]{1,0:T(8,128)} custom-call(s32[33]{0:T(128)S(1)} %pad_add_fusion.origin, s32[256]{0:T(256)S(1)} %get-tuple-element.20.places, f32[2048,128]{1,0:T(8,128)S(1)} %get-tuple-element.21.row_part, f32[1,2048]{1,0:T(1,128)S(1)} %bitcast.10, bf16[2048,1024]{1,0:T(8,128)(2,1)S(1)} %get-tuple-element.32.held, ...), custom_call_target="tpu_custom_call" | custom-call | flops 1 | bytes 8388608 | tf_op jit(solution)/shard_map/pallas_call | solution.py:218
  (26 shorter events, 0.5 us)
Async XLA Ops:
  0.0 27.0 %copy-start = (bf16[256,2048]{1,0:T(8,128)(2,1)S(1)}, bf16[256,2048]{1,0:T(8,128)(2,1)}, u32[]{:S(2)}) copy-start(bf16[256,2048]{1,0:T(8,128)(2,1)} %refs_2_.7) | copy-start | bytes 3145732
  0.0 18.4 %collective-permute-start.1 = (bf16[256,2048]{1,0:T(8,128)(2,1)}, bf16[256,2048]{1,0:T(8,128)(2,1)S(1)}, u32[]{:S(2)}, u32[]{:S(2)}) collective-permute-start(bf16[256,2048]{1,0:T(8,128)(2,1)} %refs_2_.7), channel_id=1, source_target_pairs={{0,32},{1,33},{2,34},{3,35},{4,36},{5,37},{6,38},{7,39},{8,40},{9,... | collective-permute-start | bytes 3145736 | tf_op jit(solution)/shard_map/ppermute | solution.py:43
  0.0 7.8 %collective-permute-start = (bf16[64,1024]{1,0:T(8,128)(2,1)}, bf16[64,1024]{1,0:T(8,128)(2,1)S(1)}, u32[]{:S(2)}, u32[]{:S(2)}) collective-permute-start(bf16[64,1024]{1,0:T(8,128)(2,1)} %source.1), channel_id=1, source_target_pairs={{0,1},{1,0},{2,3},{3,2},{4,5},{5,4},{6,7},{7,6},{8,9},{9,8},{10,11... | collective-permute-start | bytes 393224 | tf_op jit(solution)/shard_map/ppermute | solution.py:43
  1.7 0.9 %copy-start.1 = (bf16[64,1024]{1,0:T(8,128)(2,1)S(1)}, bf16[64,1024]{1,0:T(8,128)(2,1)}, u32[]{:S(2)}) copy-start(bf16[64,1024]{1,0:T(8,128)(2,1)} %source.1) | copy-start | bytes 393220
  2.7 33.6 %collective-permute-start.11 = (bf16[256,2048]{1,0:T(8,128)(2,1)}, bf16[256,2048]{1,0:T(8,128)(2,1)S(1)}, u32[]{:S(2)}, u32[]{:S(2)}) collective-permute-start(bf16[256,2048]{1,0:T(8,128)(2,1)} %refs_2_.7), channel_id=1, source_target_pairs={{0,64},{1,65},{2,66},{3,67},{4,68},{5,69},{6,70},{7,71},{8,72},{9,... | collective-permute-start | bytes 3145736 | tf_op jit(solution)/shard_map/ppermute | solution.py:43
  7.9 10.5 %collective-permute-start.2 = (bf16[128,1024]{1,0:T(8,128)(2,1)S(1)}, bf16[128,1024]{1,0:T(8,128)(2,1)S(1)}, u32[]{:S(2)}, u32[]{:S(2)}) collective-permute-start(bf16[128,1024]{1,0:T(8,128)(2,1)S(1)} %shard_map.93.first), channel_id=1, source_target_pairs={{0,2},{1,3},{2,4},{3,5},{4,6},{5,7},{6,0},{7,1},{8,10},{9,11},{10,... | collective-permute-start | bytes 786440 | tf_op jit(solution)/shard_map/ppermute | solution.py:43
  9.5 8.9 %collective-permute-start.5 = (bf16[128,1024]{1,0:T(8,128)(2,1)S(1)}, bf16[128,1024]{1,0:T(8,128)(2,1)S(1)}, u32[]{:S(2)}, u32[]{:S(2)}) collective-permute-start(bf16[128,1024]{1,0:T(8,128)(2,1)S(1)} %shard_map.93.first), channel_id=1, source_target_pairs={{0,6},{1,7},{2,0},{3,1},{4,2},{5,3},{6,4},{7,5},{8,14},{9,15},{10,... | collective-permute-start | bytes 786440 | tf_op jit(solution)/shard_map/ppermute | solution.py:43
  11.2 8.4 %collective-permute-start.6 = (bf16[128,1024]{1,0:T(8,128)(2,1)S(1)}, bf16[128,1024]{1,0:T(8,128)(2,1)S(1)}, u32[]{:S(2)}, u32[]{:S(2)}) collective-permute-start(bf16[128,1024]{1,0:T(8,128)(2,1)S(1)} %shard_map.93.first), channel_id=1, source_target_pairs={{0,4},{1,5},{2,6},{3,7},{4,0},{5,1},{6,2},{7,3},{8,12},{9,13},{10,... | collective-permute-start | bytes 786440 | tf_op jit(solution)/shard_map/ppermute | solution.py:43
  14.3 0.7 %copy-start.2 = (s32[1024]{0:T(1024)S(1)}, s32[1024]{0:T(1024)}, u32[]{:S(2)}) copy-start(s32[1024]{0:T(1024)} %block_place.1) | copy-start | bytes 12292
  19.6 10.8 %collective-permute-start.7 = (bf16[256,1024]{1,0:T(8,128)(2,1)S(1)}, bf16[256,1024]{1,0:T(8,128)(2,1)S(1)}, u32[]{:S(2)}, u32[]{:S(2)}) collective-permute-start(bf16[256,1024]{1,0:T(8,128)(2,1)S(1)} %shard_map.95.refs_1_), channel_id=1, source_target_pairs={{0,24},{1,25},{2,26},{3,27},{4,28},{5,29},{6,30},{7,31},{8,0},{9,1... | collective-permute-start | bytes 1572872 | tf_op jit(solution)/shard_map/ppermute | solution.py:43
  23.7 10.4 %collective-permute-start.3 = (bf16[256,1024]{1,0:T(8,128)(2,1)S(1)}, bf16[256,1024]{1,0:T(8,128)(2,1)S(1)}, u32[]{:S(2)}, u32[]{:S(2)}) collective-permute-start(bf16[256,1024]{1,0:T(8,128)(2,1)S(1)} %shard_map.94.refs_0_), channel_id=1, source_target_pairs={{0,8},{1,9},{2,10},{3,11},{4,12},{5,13},{6,14},{7,15},{8,16},{9,17... | collective-permute-start | bytes 1572872 | tf_op jit(solution)/shard_map/ppermute | solution.py:43
  23.7 16.0 %collective-permute-start.9 = (bf16[256,1024]{1,0:T(8,128)(2,1)S(1)}, bf16[256,1024]{1,0:T(8,128)(2,1)S(1)}, u32[]{:S(2)}, u32[]{:S(2)}) collective-permute-start(bf16[256,1024]{1,0:T(8,128)(2,1)S(1)} %shard_map.95.refs_1_), channel_id=1, source_target_pairs={{0,8},{1,9},{2,10},{3,11},{4,12},{5,13},{6,14},{7,15},{8,16},{9,17... | collective-permute-start | bytes 1572872 | tf_op jit(solution)/shard_map/ppermute | solution.py:43
  23.7 12.6 %collective-permute-start.10 = (bf16[256,1024]{1,0:T(8,128)(2,1)S(1)}, bf16[256,1024]{1,0:T(8,128)(2,1)S(1)}, u32[]{:S(2)}, u32[]{:S(2)}) collective-permute-start(bf16[256,1024]{1,0:T(8,128)(2,1)S(1)} %shard_map.94.refs_0_), channel_id=1, source_target_pairs={{0,24},{1,25},{2,26},{3,27},{4,28},{5,29},{6,30},{7,31},{8,0},{9,1... | collective-permute-start | bytes 1572872 | tf_op jit(solution)/shard_map/ppermute | solution.py:43
  30.4 11.6 %collective-permute-start.8 = (bf16[256,1024]{1,0:T(8,128)(2,1)S(1)}, bf16[256,1024]{1,0:T(8,128)(2,1)S(1)}, u32[]{:S(2)}, u32[]{:S(2)}) collective-permute-start(bf16[256,1024]{1,0:T(8,128)(2,1)S(1)} %collective-permute-done.7.refs_1_), channel_id=1, source_target_pairs={{0,24},{1,25},{2,26},{3,27},{4,28},{5,29},{6,30},{7,31},{8,0},{9,1... | collective-permute-start | bytes 1572872 | tf_op jit(solution)/shard_map/ppermute | solution.py:43
  34.1 11.2 %collective-permute-start.4 = (bf16[256,1024]{1,0:T(8,128)(2,1)S(1)}, bf16[256,1024]{1,0:T(8,128)(2,1)S(1)}, u32[]{:S(2)}, u32[]{:S(2)}) collective-permute-start(bf16[256,1024]{1,0:T(8,128)(2,1)S(1)} %collective-permute-done.3.refs_0_), channel_id=1, source_target_pairs={{0,8},{1,9},{2,10},{3,11},{4,12},{5,13},{6,14},{7,15},{8,16},{9,17... | collective-permute-start | bytes 1572872 | tf_op jit(solution)/shard_map/ppermute | solution.py:43
  41.9 5.6 %collective-permute-start.12 = (bf16[256,2048]{1,0:T(8,128)(2,1)S(1)}, bf16[256,2048]{1,0:T(8,128)(2,1)S(1)}, u32[]{:S(2)}, u32[]{:S(2)}) collective-permute-start(bf16[256,2048]{1,0:T(8,128)(2,1)S(1)} %collective-permute-done.11.refs_6_.across), channel_id=1, source_target_pairs={{0,32},{1,33},{2,34},{3,35},{4,36},{5,37},{6,38},{7,39},{8,40},{9,... | collective-permute-start | bytes 3145736 | tf_op jit(solution)/shard_map/ppermute | solution.py:43

commit v3 on v2

--- a/solution.py
+++ b/solution.py
@@ -13,6 +13,7 @@
 RING = 4
 PIECE = 256
 TILE = 256
+STEP = 16
 
 
 def move(target):
@@ -84,17 +85,35 @@
     )(first, second)
 
 
-def arrange(origin, block_place, row_term, row_part, places):
-    grid_row = origin[32]
-
-    def block(i, carry):
-        place = block_place[origin[i // BLK] * BLK + i % BLK] - grid_row * 256
-        places[i] = place
-        at, to = pl.multiple_of(place * BLK, BLK), pl.multiple_of(i * BLK, BLK)
-        row_part[pl.ds(to, BLK), :] = row_term[pl.ds(at, BLK), :]
+def places_of(origin, block_place, group):
+    shards = [origin[group * (STEP // BLK) + j] * BLK for j in range(STEP // BLK)]
+    start = origin[32] * 256
+    return [block_place[shards[j // BLK] + j % BLK] - start for j in range(STEP)]
+
+
+def arrange(origin, block_place, row_term, row_part):
+    def some(group, carry):
+        at = [pl.multiple_of(place * BLK, BLK) for place in places_of(origin, block_place, group)]
+        terms = [row_term[pl.ds(place, BLK), :] for place in at]
+        for j, term in enumerate(terms):
+            to = pl.multiple_of((group * STEP + j) * BLK, BLK)
+            row_part[pl.ds(to, BLK), :] = term
         return carry
 
-    lax.fori_loop(0, 256, block, 0, unroll=8)
+    lax.fori_loop(0, 256 // STEP, some, 0)
+
+
+def list_places(origin, block_place, places):
+    def some(group, carry):
+        for j, place in enumerate(places_of(origin, block_place, group)):
+            places[group * STEP + j] = place
+        return carry
+
+    lax.fori_loop(0, 256 // STEP, some, 0)
+
+
+def stand(places, across, sums, mark):
+    mark[...] = jnp.zeros_like(mark)
 
 
 def begin(pair, origin, *refs):
@@ -182,15 +201,35 @@
 def arranged(origin, block_place, row_term):
     return pl.pallas_call(
         arrange,
-        out_shape=[
-            jax.ShapeDtypeStruct(row_term.shape, jnp.float32),
-            jax.ShapeDtypeStruct((256,), jnp.int32),
-        ],
+        out_shape=jax.ShapeDtypeStruct(row_term.shape, jnp.float32),
         in_specs=[SMEM, SMEM, VMEM],
-        out_specs=[VMEM, SMEM],
+        out_specs=VMEM,
         compiler_params=limits(4),
-        cost_estimate=cost(0, 2**21),
+        cost_estimate=cost(3 * 10**9, 2**21),
     )(origin, block_place, row_term)
+
+
+def listed(origin, block_place):
+    return pl.pallas_call(
+        list_places,
+        out_shape=jax.ShapeDtypeStruct((256,), jnp.int32),
+        in_specs=[SMEM, SMEM],
+        out_specs=SMEM,
+        compiler_params=limits(1),
+        cost_estimate=cost(10**9, 2**20),
+    )(origin, block_place)
+
+
+def stood(places, across, sums):
+    anywhere = pl.BlockSpec(memory_space=pl.ANY)
+    return pl.pallas_call(
+        stand,
+        out_shape=jax.ShapeDtypeStruct((8, 128), jnp.float32),
+        in_specs=[SMEM, anywhere, anywhere],
+        out_specs=VMEM,
+        compiler_params=limits(1),
+        cost_estimate=cost(5 * 10**9, 2**12),
+    )(places, across, sums)
 
 
 def begun(pair, work, origin, pieces, own, beside, so_far, *awaited):
@@ -264,10 +303,11 @@
     col_term = (col_occ[:, None] - vir_eff[None, :]).reshape(1, col_dev)
 
     own = load(t_store)
-    pair = join(own, send(t_store, ACROSS_LO))
-    beside = send(w_panels, OTHER_CORE)
-    row_part, places = arranged(origin, block_place, row_term)
-    near = join(after(pair, row_part, places, col_term, beside), send(pair, along_first(1)))
+    fetched = send(t_store, ACROSS_LO)
+    pair = join(after(own, row_term, col_term), fetched)
+    row_part = arranged(origin, block_place, row_term)
+    beside = send(after(w_panels, pair), OTHER_CORE)
+    near = join(after(pair, beside), send(pair, along_first(1)))
     far = join(after(send(pair, along_first(-1)), near), send(pair, along_first(2)))
     near_up = send(near, along_second(1))
     far_down = send(far, along_second(-1))
@@ -276,12 +316,14 @@
     near_two = send(near_up, along_second(1))
     far_two = send(far_down, along_second(-1))
 
-    across = send(after(w_panels, own), ACROSS_HI)
-    so_far = begun(0, int(3 * 10**9), origin, (near, far), w_panels, beside, [])
-    so_far = begun(1, int(3 * 10**9), origin, (near_up, far_down), w_panels, beside, so_far)
-    so_far = begun(2, int(3 * 10**9), origin, (far_up, near_down), w_panels, beside, so_far, across)
-    aslant = send(after(across, so_far[1]), OTHER_CORE)
-    held, sums = begun(3, 12 * 10**9, origin, (near_two, far_two), w_panels, beside, so_far)
+    across = send(after(w_panels, fetched), ACROSS_HI)
+    so_far = begun(0, 3 * 10**9, origin, (near, far), w_panels, beside, [])
+    so_far = begun(1, 3 * 10**9, origin, (near_up, far_down), w_panels, beside, so_far)
+    so_far = begun(2, 1 * 10**9, origin, (far_up, near_down), w_panels, beside, so_far, row_part)
+    places = listed(origin, block_place)
+    mark = stood(places, across, so_far[1])
+    aslant = send(after(across, mark), OTHER_CORE)
+    held, sums = begun(3, 12 * 10**9, origin, (near_two, far_two), w_panels, beside, so_far, mark)
     return finished(origin, places, row_part, col_term, held, sums, across, aslant)
 
 

time: 57.1 us -> 54.5 us (0.954)
  waiting for transfers between devices: 9.04 us -> 5.72 us
    ppermute x13, waiting for transfers between devices: 9.04 us -> 5.72 us  [send(): return lax.ppermute(value, ('row', 'col'), pairs)]
    pallas_call x1 -> x3, Pallas kernels: 3.39 us -> 3.23 us  [the longest x1 1.63 us: listed(): pl.pallas_call(list_places, out_shape=jax.ShapeDtypeStruct((256,), jnp.in...]
  transfers between devices with their start and end apart: 13 -> 13, of which waited for: 4 -> 4; matrix products, arithmetic and copies ran while one was open for 6% -> 6% of each run, Pallas kernels for 22% -> 23%
where the time goes in v3:
time: 54.5 us; the launch traced here: 53.9 us
  Pallas kernels  21.6 us (40%)
  starting transfers between devices  21.3 us (39%)
  waiting for transfers between devices  5.72 us (10%)
  local copies, waits for them, and re-layouts  2.78 us (5%)
  other arithmetic  2.21 us (4%)
    ppermute x13, starting transfers between devices, send(): return lax.ppermute(value, ('row', 'col'), pairs)  21.3 us
    pallas_call x1, Pallas kernels, finished(): pl.pallas_call(finish, out_shape=jax.ShapeDtypeStruct(shape, jnp.float32)...  9.28 us
    pallas_call x4, Pallas kernels, begun(): pl.pallas_call(functools.partial(begin, pair), out_shape=shapes, in_specs...  8.84 us
    ppermute x13, waiting for transfers between devices, send(): return lax.ppermute(value, ('row', 'col'), pairs)  5.72 us
    unnamed x8, local copies, waits for them, and re-layouts  1.64 us
    pallas_call x1, Pallas kernels, listed(): pl.pallas_call(list_places, out_shape=jax.ShapeDtypeStruct((256,), jnp.in...  1.63 us
    reduce_sum x1, other arithmetic, per_device(): jnp.sum(jnp.where(vir_order[:, None] == indices[None, :], vir_energy[None...  1.36 us
  transfers between devices with their start and end apart: 13, of which 4 were waited for; matrix products, arithmetic and copies ran while one was open for 6% of the time, Pallas kernels for 23%

profile of v3, /device:TPU:0, one launch (start us, length us, event | category | flops | bytes accessed | tf_op | source)
XLA Modules:
  0.0 53.9 jit_solution(15719658008439413215)
XLA Ops:
  0.0 1.6 %collective-permute-start = (bf16[64,1024]{1,0:T(8,128)(2,1)}, bf16[64,1024]{1,0:T(8,128)(2,1)S(1)}, u32[]{:S(2)}, u32[]{:S(2)}) collective-permute-start(bf16[64,1024]{1,0:T(8,128)(2,1)} %source.1), channel_id=1, source_target_pairs={{0,1},{1,0},{2,3},{3,2},{4,5},{5,4},{6,7},{7,6},{8,9},{9,8},{10,11... | collective-permute-start | bytes 393224 | tf_op jit(solution)/shard_map/ppermute | solution.py:44
  1.6 0.9 %copy-done.1 = bf16[64,1024]{1,0:T(8,128)(2,1)S(1)} copy-done((bf16[64,1024]{1,0:T(8,128)(2,1)S(1)}, bf16[64,1024]{1,0:T(8,128)(2,1)}, u32[]{:S(2)}) %copy-start.1) | copy-done | bytes 131096
  2.7 1.4 %select_reduce_fusion = f32[1024]{0:T(1024)S(1)} fusion(f32[1024]{0:T(1024)} %param.13, s32[1024]{0:T(1024)} %param.14), kind=kLoop, calls=%fused_computation | loop fusion | flops 3144704 | bytes 12288 | tf_op jit(solution)/shard_map/reduce_sum | solution.py:295
  4.0 0.8 %fusion.7 = (f32[2]{0:T(128)S(1)}, f32[2]{0:T(128)S(1)}) fusion(f32[64]{0:T(128)} %param.12, s32[]{:T(128)S(6)} %select_n.74, s32[]{:T(128)S(6)} %select_n.72), kind=kLoop, calls=%fused_computation.21 | loop fusion | bytes 40 | tf_op jit(solution)/shard_map/dynamic_slice | solution.py:299
  5.5 1.9 %collective-permute-start.2 = (bf16[128,1024]{1,0:T(8,128)(2,1)S(1)}, bf16[128,1024]{1,0:T(8,128)(2,1)S(1)}, u32[]{:S(2)}, u32[]{:S(2)}) collective-permute-start(bf16[128,1024]{1,0:T(8,128)(2,1)S(1)} %shard_map.94.first), channel_id=1, source_target_pairs={{0,2},{1,3},{2,4},{3,5},{4,6},{5,7},{6,0},{7,1},{8,10},{9,11},{10,... | collective-permute-start | bytes 786440 | tf_op jit(solution)/shard_map/ppermute | solution.py:44
  7.4 1.5 %collective-permute-start.5 = (bf16[128,1024]{1,0:T(8,128)(2,1)S(1)}, bf16[128,1024]{1,0:T(8,128)(2,1)S(1)}, u32[]{:S(2)}, u32[]{:S(2)}) collective-permute-start(bf16[128,1024]{1,0:T(8,128)(2,1)S(1)} %shard_map.94.first), channel_id=1, source_target_pairs={{0,6},{1,7},{2,0},{3,1},{4,2},{5,3},{6,4},{7,5},{8,14},{9,15},{10,... | collective-permute-start | bytes 786440 | tf_op jit(solution)/shard_map/ppermute | solution.py:44
  8.9 2.1 %collective-permute-start.6 = (bf16[128,1024]{1,0:T(8,128)(2,1)S(1)}, bf16[128,1024]{1,0:T(8,128)(2,1)S(1)}, u32[]{:S(2)}, u32[]{:S(2)}) collective-permute-start(bf16[128,1024]{1,0:T(8,128)(2,1)S(1)} %shard_map.94.first), channel_id=1, source_target_pairs={{0,4},{1,5},{2,6},{3,7},{4,0},{5,1},{6,2},{7,3},{8,12},{9,13},{10,... | collective-permute-start | bytes 786440 | tf_op jit(solution)/shard_map/ppermute | solution.py:44
  11.0 0.7 %fusion.6 = s32[32]{0:T(128)S(1)} fusion(s32[32]{0:T(128)} %constant.86.clone, s32[32]{0:T(128)} %constant.87.clone, pred[]{:T(512)S(6)} %eq.26, s32[32]{0:T(128)} %constant.88.clone, s32[]{:T(128)S(6)} %select_n.71, s32[]{:T(128)S(6)} %select_n.67, s32[]{:T(128)S(6)} %select_n.65, s32[]{:T(128)S(6)} %mul.21), kind=kLoop, calls=%fused_computation.19 | loop fusion | flops 1024 | bytes 529 | tf_op jit(solution)/shard_map/add | solution.py:291
  11.7 3.1 %collective-permute-start.11 = (bf16[256,2048]{1,0:T(8,128)(2,1)}, bf16[256,2048]{1,0:T(8,128)(2,1)S(1)}, u32[]{:S(2)}, u32[]{:S(2)}) collective-permute-start(bf16[256,2048]{1,0:T(8,128)(2,1)} %refs_2_.7), channel_id=1, source_target_pairs={{0,64},{1,65},{2,66},{3,67},{4,68},{5,69},{6,70},{7,71},{8,72},{9,... | collective-permute-start | bytes 3145736 | tf_op jit(solution)/shard_map/ppermute | solution.py:44
  14.9 0.7 %copy-done.2 = s32[1024]{0:T(1024)S(1)} copy-done((s32[1024]{0:T(1024)S(1)}, s32[1024]{0:T(1024)}, u32[]{:S(2)}) %copy-start.2) | copy-done | bytes 4120
  15.6 1.6 %shard_map.91.places = s32[256]{0:T(256)S(1)} custom-call(s32[33]{0:T(128)S(1)} %pad_add_fusion.origin, s32[1024]{0:T(1024)S(1)} %copy-done.2), custom_call_target="tpu_custom_call" | custom-call | flops 1000000000 | bytes 1048576 | tf_op jit(solution)/shard_map/pallas_call | solution.py:213
  17.3 2.0 %collective-permute-start.3 = (bf16[256,1024]{1,0:T(8,128)(2,1)S(1)}, bf16[256,1024]{1,0:T(8,128)(2,1)S(1)}, u32[]{:S(2)}, u32[]{:S(2)}) collective-permute-start(bf16[256,1024]{1,0:T(8,128)(2,1)S(1)} %shard_map.95.refs_0_), channel_id=1, source_target_pairs={{0,8},{1,9},{2,10},{3,11},{4,12},{5,13},{6,14},{7,15},{8,16},{9,17... | collective-permute-start | bytes 1572872 | tf_op jit(solution)/shard_map/ppermute | solution.py:44
  19.3 2.3 %collective-permute-start.7 = (bf16[256,1024]{1,0:T(8,128)(2,1)S(1)}, bf16[256,1024]{1,0:T(8,128)(2,1)S(1)}, u32[]{:S(2)}, u32[]{:S(2)}) collective-permute-start(bf16[256,1024]{1,0:T(8,128)(2,1)S(1)} %shard_map.96.refs_1_), channel_id=1, source_target_pairs={{0,24},{1,25},{2,26},{3,27},{4,28},{5,29},{6,30},{7,31},{8,0},{9,1... | collective-permute-start | bytes 1572872 | tf_op jit(solution)/shard_map/ppermute | solution.py:44
  21.6 1.1 %shard_map.92.refs_6_.row_part = f32[2048,128]{1,0:T(8,128)S(1)} custom-call(s32[33]{0:T(128)S(1)} %pad_add_fusion.origin, s32[1024]{0:T(1024)S(1)} %copy-done.2, f32[2048,128]{1,0:T(8,128)S(1)} %broadcast_in_dim.30.row_term), custom_call_target="tpu_custom_call" | custom-call | flops 3000000000 | bytes 2097152 | tf_op jit(solution)/shard_map/pallas_call | solution.py:202
  22.7 3.2 %collective-permute-start.10 = (bf16[256,1024]{1,0:T(8,128)(2,1)S(1)}, bf16[256,1024]{1,0:T(8,128)(2,1)S(1)}, u32[]{:S(2)}, u32[]{:S(2)}) collective-permute-start(bf16[256,1024]{1,0:T(8,128)(2,1)S(1)} %shard_map.95.refs_0_), channel_id=1, source_target_pairs={{0,24},{1,25},{2,26},{3,27},{4,28},{5,29},{6,30},{7,31},{8,0},{9,1... | collective-permute-start | bytes 1572872 | tf_op jit(solution)/shard_map/ppermute | solution.py:44
  25.9 2.2 %shard_map.97 = (bf16[2048,1024]{1,0:T(8,128)(2,1)S(1)}, f32[2048,2048]{1,0:T(8,128)S(1)}) custom-call(s32[33]{0:T(128)S(1)} %pad_add_fusion.origin, bf16[256,1024]{1,0:T(8,128)(2,1)S(1)} %shard_map.95.refs_0_, bf16[256,1024]{1,0:T(8,128)(2,1)S(1)} %shard_map.96.refs_1_, bf16[256,2048]{1,0:T(8,128)(2,1)S(1)} %copy-done, ...), custom_call_target="tpu_custom_call" | custom-call | flops 3000000000 | bytes 2097152 | tf_op jit(solution)/shard_map/pallas_call | solution.py:242
  28.6 3.4 %collective-permute-start.8 = (bf16[256,1024]{1,0:T(8,128)(2,1)S(1)}, bf16[256,1024]{1,0:T(8,128)(2,1)S(1)}, u32[]{:S(2)}, u32[]{:S(2)}) collective-permute-start(bf16[256,1024]{1,0:T(8,128)(2,1)S(1)} %collective-permute-done.7.refs_1_), channel_id=1, source_target_pairs={{0,24},{1,25},{2,26},{3,27},{4,28},{5,29},{6,30},{7,31},{8,0},{9,1... | collective-permute-start | bytes 1572872 | tf_op jit(solution)/shard_map/ppermute | solution.py:44
  32.0 2.2 %shard_map.98 = (bf16[2048,1024]{1,0:T(8,128)(2,1)S(1)}, f32[2048,2048]{1,0:T(8,128)S(1)}) custom-call(s32[33]{0:T(128)S(1)} %pad_add_fusion.origin, bf16[256,1024]{1,0:T(8,128)(2,1)S(1)} %collective-permute-done.3.refs_0_, bf16[256,1024]{1,0:T(8,128)(2,1)S(1)} %collective-permute-done.7.refs_1_, ...), custom_call_target="tpu_custom_call", output_to_operand_aliasing={{0}: (5, {}), {1}: (6, {})} | custom-call | flops 3000000000 | bytes 2097152 | tf_op jit(solution)/shard_map/pallas_call | solution.py:242
  34.2 2.2 %shard_map.99 = (bf16[2048,1024]{1,0:T(8,128)(2,1)S(1)}, f32[2048,2048]{1,0:T(8,128)S(1)}) custom-call(s32[33]{0:T(128)S(1)} %pad_add_fusion.origin, bf16[256,1024]{1,0:T(8,128)(2,1)S(1)} %collective-permute-done.9.refs_0_, bf16[256,1024]{1,0:T(8,128)(2,1)S(1)} %collective-permute-done.10.refs_1_, ...), custom_call_target="tpu_custom_call", output_to_operand_aliasing={{0}: (5, {}), {1}: (6, {})} | custom-call | flops 1000000000 | bytes 2097152 | tf_op jit(solution)/shard_map/pallas_call | solution.py:242
  36.4 2.3 %collective-permute-done.11.across = bf16[256,2048]{1,0:T(8,128)(2,1)S(1)} collective-permute-done((bf16[256,2048]{1,0:T(8,128)(2,1)}, bf16[256,2048]{1,0:T(8,128)(2,1)S(1)}, u32[]{:S(2)}, u32[]{:S(2)}) %collective-permute-start.11) | collective-permute-done | bytes 1048608 | tf_op jit(solution)/shard_map/ppermute | solution.py:44
  38.8 0.5 %shard_map.100.refs_6_ = f32[8,128]{1,0:T(8,128)S(1)} custom-call(s32[256]{0:T(256)S(1)} %shard_map.91.places, bf16[256,2048]{1,0:T(8,128)(2,1)S(1)} %collective-permute-done.11.across, f32[2048,2048]{1,0:T(8,128)S(1)} %get-tuple-element.30.sums.refs_5_), custom_call_target="tpu_custom_call" | custom-call | flops 5000000000 | bytes 4096 | tf_op jit(solution)/shard_map/pallas_call | solution.py:225
  39.8 2.6 %collective-permute-done.4.refs_0_ = bf16[256,1024]{1,0:T(8,128)(2,1)S(1)} collective-permute-done((bf16[256,1024]{1,0:T(8,128)(2,1)S(1)}, bf16[256,1024]{1,0:T(8,128)(2,1)S(1)}, u32[]{:S(2)}, u32[]{:S(2)}) %collective-permute-start.4) | collective-permute-done | bytes 524320 | tf_op jit(solution)/shard_map/ppermute | solution.py:44
  42.4 2.2 %shard_map.101 = (bf16[2048,1024]{1,0:T(8,128)(2,1)S(1)}, f32[2048,2048]{1,0:T(8,128)S(1)}) custom-call(s32[33]{0:T(128)S(1)} %pad_add_fusion.origin, bf16[256,1024]{1,0:T(8,128)(2,1)S(1)} %collective-permute-done.4.refs_0_, bf16[256,1024]{1,0:T(8,128)(2,1)S(1)} %collective-permute-done.8.refs_1_, ...), custom_call_target="tpu_custom_call", output_to_operand_aliasing={{0}: (5, {}), {1}: (6, {})} | custom-call | flops 12000000000 | bytes 2097152 | tf_op jit(solution)/shard_map/pallas_call | solution.py:242
  44.6 9.3 %shard_map.102 = f32[2048,2048]{1,0:T(8,128)} custom-call(s32[33]{0:T(128)S(1)} %pad_add_fusion.origin, s32[256]{0:T(256)S(1)} %shard_map.91.places, f32[2048,128]{1,0:T(8,128)S(1)} %shard_map.92.refs_6_.row_part, f32[1,2048]{1,0:T(1,128)S(1)} %bitcast.10, bf16[2048,1024]{1,0:T(8,128)(2,1)S(1)} %get-tuple-element.32.held, ...), custom_call_target="tpu_custom_call" | custom-call | flops 1 | bytes 8388608 | tf_op jit(solution)/shard_map/pallas_call | solution.py:257
  (28 shorter events, 1.8 us)
Async XLA Ops:
  0.0 5.3 %collective-permute-start = (bf16[64,1024]{1,0:T(8,128)(2,1)}, bf16[64,1024]{1,0:T(8,128)(2,1)S(1)}, u32[]{:S(2)}, u32[]{:S(2)}) collective-permute-start(bf16[64,1024]{1,0:T(8,128)(2,1)} %source.1), channel_id=1, source_target_pairs={{0,1},{1,0},{2,3},{3,2},{4,5},{5,4},{6,7},{7,6},{8,9},{9,8},{10,11... | collective-permute-start | bytes 393224 | tf_op jit(solution)/shard_map/ppermute | solution.py:44
  1.6 0.9 %copy-start.1 = (bf16[64,1024]{1,0:T(8,128)(2,1)S(1)}, bf16[64,1024]{1,0:T(8,128)(2,1)}, u32[]{:S(2)}) copy-start(bf16[64,1024]{1,0:T(8,128)(2,1)} %source.1) | copy-start | bytes 393220
  5.3 11.9 %collective-permute-start.1 = (bf16[256,2048]{1,0:T(8,128)(2,1)}, bf16[256,2048]{1,0:T(8,128)(2,1)S(1)}, u32[]{:S(2)}, u32[]{:S(2)}) collective-permute-start(bf16[256,2048]{1,0:T(8,128)(2,1)} %refs_2_.7), channel_id=1, source_target_pairs={{0,32},{1,33},{2,34},{3,35},{4,36},{5,37},{6,38},{7,39},{8,40},{9,... | collective-permute-start | bytes 3145736 | tf_op jit(solution)/shard_map/ppermute | solution.py:44
  5.5 11.8 %collective-permute-start.2 = (bf16[128,1024]{1,0:T(8,128)(2,1)S(1)}, bf16[128,1024]{1,0:T(8,128)(2,1)S(1)}, u32[]{:S(2)}, u32[]{:S(2)}) collective-permute-start(bf16[128,1024]{1,0:T(8,128)(2,1)S(1)} %shard_map.94.first), channel_id=1, source_target_pairs={{0,2},{1,3},{2,4},{3,5},{4,6},{5,7},{6,0},{7,1},{8,10},{9,11},{10,... | collective-permute-start | bytes 786440 | tf_op jit(solution)/shard_map/ppermute | solution.py:44
  7.4 11.9 %collective-permute-start.5 = (bf16[128,1024]{1,0:T(8,128)(2,1)S(1)}, bf16[128,1024]{1,0:T(8,128)(2,1)S(1)}, u32[]{:S(2)}, u32[]{:S(2)}) collective-permute-start(bf16[128,1024]{1,0:T(8,128)(2,1)S(1)} %shard_map.94.first), channel_id=1, source_target_pairs={{0,6},{1,7},{2,0},{3,1},{4,2},{5,3},{6,4},{7,5},{8,14},{9,15},{10,... | collective-permute-start | bytes 786440 | tf_op jit(solution)/shard_map/ppermute | solution.py:44
  8.9 10.4 %collective-permute-start.6 = (bf16[128,1024]{1,0:T(8,128)(2,1)S(1)}, bf16[128,1024]{1,0:T(8,128)(2,1)S(1)}, u32[]{:S(2)}, u32[]{:S(2)}) collective-permute-start(bf16[128,1024]{1,0:T(8,128)(2,1)S(1)} %shard_map.94.first), channel_id=1, source_target_pairs={{0,4},{1,5},{2,6},{3,7},{4,0},{5,1},{6,2},{7,3},{8,12},{9,13},{10,... | collective-permute-start | bytes 786440 | tf_op jit(solution)/shard_map/ppermute | solution.py:44
  11.7 27.1 %collective-permute-start.11 = (bf16[256,2048]{1,0:T(8,128)(2,1)}, bf16[256,2048]{1,0:T(8,128)(2,1)S(1)}, u32[]{:S(2)}, u32[]{:S(2)}) collective-permute-start(bf16[256,2048]{1,0:T(8,128)(2,1)} %refs_2_.7), channel_id=1, source_target_pairs={{0,64},{1,65},{2,66},{3,67},{4,68},{5,69},{6,70},{7,71},{8,72},{9,... | collective-permute-start | bytes 3145736 | tf_op jit(solution)/shard_map/ppermute | solution.py:44
  14.9 0.7 %copy-start.2 = (s32[1024]{0:T(1024)S(1)}, s32[1024]{0:T(1024)}, u32[]{:S(2)}) copy-start(s32[1024]{0:T(1024)} %block_place.3) | copy-start | bytes 12292
  17.3 14.7 %collective-permute-start.3 = (bf16[256,1024]{1,0:T(8,128)(2,1)S(1)}, bf16[256,1024]{1,0:T(8,128)(2,1)S(1)}, u32[]{:S(2)}, u32[]{:S(2)}) collective-permute-start(bf16[256,1024]{1,0:T(8,128)(2,1)S(1)} %shard_map.95.refs_0_), channel_id=1, source_target_pairs={{0,8},{1,9},{2,10},{3,11},{4,12},{5,13},{6,14},{7,15},{8,16},{9,17... | collective-permute-start | bytes 1572872 | tf_op jit(solution)/shard_map/ppermute | solution.py:44
  19.3 6.6 %copy-start = (bf16[256,2048]{1,0:T(8,128)(2,1)S(1)}, bf16[256,2048]{1,0:T(8,128)(2,1)}, u32[]{:S(2)}) copy-start(bf16[256,2048]{1,0:T(8,128)(2,1)} %refs_2_.7) | copy-start | bytes 3145732
  19.3 9.3 %collective-permute-start.7 = (bf16[256,1024]{1,0:T(8,128)(2,1)S(1)}, bf16[256,1024]{1,0:T(8,128)(2,1)S(1)}, u32[]{:S(2)}, u32[]{:S(2)}) collective-permute-start(bf16[256,1024]{1,0:T(8,128)(2,1)S(1)} %shard_map.96.refs_1_), channel_id=1, source_target_pairs={{0,24},{1,25},{2,26},{3,27},{4,28},{5,29},{6,30},{7,31},{8,0},{9,1... | collective-permute-start | bytes 1572872 | tf_op jit(solution)/shard_map/ppermute | solution.py:44
  22.6 11.6 %collective-permute-start.9 = (bf16[256,1024]{1,0:T(8,128)(2,1)S(1)}, bf16[256,1024]{1,0:T(8,128)(2,1)S(1)}, u32[]{:S(2)}, u32[]{:S(2)}) collective-permute-start(bf16[256,1024]{1,0:T(8,128)(2,1)S(1)} %shard_map.96.refs_1_), channel_id=1, source_target_pairs={{0,8},{1,9},{2,10},{3,11},{4,12},{5,13},{6,14},{7,15},{8,16},{9,17... | collective-permute-start | bytes 1572872 | tf_op jit(solution)/shard_map/ppermute | solution.py:44
  22.7 11.5 %collective-permute-start.10 = (bf16[256,1024]{1,0:T(8,128)(2,1)S(1)}, bf16[256,1024]{1,0:T(8,128)(2,1)S(1)}, u32[]{:S(2)}, u32[]{:S(2)}) collective-permute-start(bf16[256,1024]{1,0:T(8,128)(2,1)S(1)} %shard_map.95.refs_0_), channel_id=1, source_target_pairs={{0,24},{1,25},{2,26},{3,27},{4,28},{5,29},{6,30},{7,31},{8,0},{9,1... | collective-permute-start | bytes 1572872 | tf_op jit(solution)/shard_map/ppermute | solution.py:44
  28.6 11.2 %collective-permute-start.8 = (bf16[256,1024]{1,0:T(8,128)(2,1)S(1)}, bf16[256,1024]{1,0:T(8,128)(2,1)S(1)}, u32[]{:S(2)}, u32[]{:S(2)}) collective-permute-start(bf16[256,1024]{1,0:T(8,128)(2,1)S(1)} %collective-permute-done.7.refs_1_), channel_id=1, source_target_pairs={{0,24},{1,25},{2,26},{3,27},{4,28},{5,29},{6,30},{7,31},{8,0},{9,1... | collective-permute-start | bytes 1572872 | tf_op jit(solution)/shard_map/ppermute | solution.py:44
  32.0 10.4 %collective-permute-start.4 = (bf16[256,1024]{1,0:T(8,128)(2,1)S(1)}, bf16[256,1024]{1,0:T(8,128)(2,1)S(1)}, u32[]{:S(2)}, u32[]{:S(2)}) collective-permute-start(bf16[256,1024]{1,0:T(8,128)(2,1)S(1)} %collective-permute-done.3.refs_0_), channel_id=1, source_target_pairs={{0,8},{1,9},{2,10},{3,11},{4,12},{5,13},{6,14},{7,15},{8,16},{9,17... | collective-permute-start | bytes 1572872 | tf_op jit(solution)/shard_map/ppermute | solution.py:44
  39.3 5.2 %collective-permute-start.12 = (bf16[256,2048]{1,0:T(8,128)(2,1)S(1)}, bf16[256,2048]{1,0:T(8,128)(2,1)S(1)}, u32[]{:S(2)}, u32[]{:S(2)}) collective-permute-start(bf16[256,2048]{1,0:T(8,128)(2,1)S(1)} %collective-permute-done.11.across), channel_id=1, source_target_pairs={{0,32},{1,33},{2,34},{3,35},{4,36},{5,37},{6,38},{7,39},{8,40},{9,... | collective-permute-start | bytes 3145736 | tf_op jit(solution)/shard_map/ppermute | solution.py:44

commit v4 on v3

--- a/solution.py
+++ b/solution.py
@@ -112,7 +112,7 @@
     lax.fori_loop(0, 256 // STEP, some, 0)
 
 
-def stand(places, across, sums, mark):
+def stand(across, sums, mark):
     mark[...] = jnp.zeros_like(mark)
 
 
@@ -220,16 +220,16 @@
     )(origin, block_place)
 
 
-def stood(places, across, sums):
+def stood(across, sums):
     anywhere = pl.BlockSpec(memory_space=pl.ANY)
     return pl.pallas_call(
         stand,
         out_shape=jax.ShapeDtypeStruct((8, 128), jnp.float32),
-        in_specs=[SMEM, anywhere, anywhere],
+        in_specs=[anywhere, anywhere],
         out_specs=VMEM,
         compiler_params=limits(1),
         cost_estimate=cost(5 * 10**9, 2**12),
-    )(places, across, sums)
+    )(across, sums)
 
 
 def begun(pair, work, origin, pieces, own, beside, so_far, *awaited):
@@ -244,7 +244,7 @@
         out_shape=shapes,
         in_specs=[SMEM]
         + [VMEM] * (len(operands) - 1 - len(awaited))
-        + [pl.BlockSpec(memory_space=pl.ANY)] * len(awaited),
+        + [SMEM if x.dtype == jnp.int32 else pl.BlockSpec(memory_space=pl.ANY) for x in awaited],
         out_specs=[VMEM, VMEM],
         input_output_aliases={5: 0, 6: 1} if so_far else {},
         compiler_params=limits(4),
@@ -317,11 +317,11 @@
     far_two = send(far_down, along_second(-1))
 
     across = send(after(w_panels, fetched), ACROSS_HI)
+    places = listed(origin, block_place)
     so_far = begun(0, 3 * 10**9, origin, (near, far), w_panels, beside, [])
-    so_far = begun(1, 3 * 10**9, origin, (near_up, far_down), w_panels, beside, so_far)
+    so_far = begun(1, 3 * 10**9, origin, (near_up, far_down), w_panels, beside, so_far, places)
     so_far = begun(2, 1 * 10**9, origin, (far_up, near_down), w_panels, beside, so_far, row_part)
-    places = listed(origin, block_place)
-    mark = stood(places, across, so_far[1])
+    mark = stood(across, so_far[1])
     aslant = send(after(across, mark), OTHER_CORE)
     held, sums = begun(3, 12 * 10**9, origin, (near_two, far_two), w_panels, beside, so_far, mark)
     return finished(origin, places, row_part, col_term, held, sums, across, aslant)

time: 54.5 us -> 54.5 us (level)
  waiting for transfers between devices: 5.72 us -> 6.36 us
    ppermute x13, waiting for transfers between devices: 5.72 us -> 6.36 us  [send(): return lax.ppermute(value, ('row', 'col'), pairs)]
    pallas_call x1, Pallas kernels: 0.55 us -> 0.01 us  [stood(): pl.pallas_call(stand, out_shape=jax.ShapeDtypeStruct((8, 128), jnp.float3...]
  transfers between devices with their start and end apart: 13 -> 13, of which waited for: 4 -> 4; matrix products, arithmetic and copies ran while one was open for 6% -> 6% of each run, Pallas kernels for 23% -> 22%
where the time goes in v4:
time: 54.5 us; the launch traced here: 53.9 us
  starting transfers between devices  21.2 us (39%)
  Pallas kernels  21.1 us (39%)
  waiting for transfers between devices  6.36 us (12%)
  local copies, waits for them, and re-layouts  2.78 us (5%)
  other arithmetic  2.21 us (4%)
    ppermute x13, starting transfers between devices, send(): return lax.ppermute(value, ('row', 'col'), pairs)  21.2 us
    pallas_call x1, Pallas kernels, finished(): pl.pallas_call(finish, out_shape=jax.ShapeDtypeStruct(shape, jnp.float32)...  9.28 us
    pallas_call x4, Pallas kernels, begun(): pl.pallas_call(functools.partial(begin, pair), out_shape=shapes, in_specs...  8.86 us
    ppermute x13, waiting for transfers between devices, send(): return lax.ppermute(value, ('row', 'col'), pairs)  6.36 us
    unnamed x8, local copies, waits for them, and re-layouts  1.64 us
    pallas_call x1, Pallas kernels, listed(): pl.pallas_call(list_places, out_shape=jax.ShapeDtypeStruct((256,), jnp.in...  1.63 us
    reduce_sum x1, other arithmetic, per_device(): jnp.sum(jnp.where(vir_order[:, None] == indices[None, :], vir_energy[None...  1.36 us
  transfers between devices with their start and end apart: 13, of which 4 were waited for; matrix products, arithmetic and copies ran while one was open for 6% of the time, Pallas kernels for 22%

profile of v4, /device:TPU:0, one launch (start us, length us, event | category | flops | bytes accessed | tf_op | source)
XLA Modules:
  0.0 53.9 jit_solution(18323232354215462692)
XLA Ops:
  0.0 1.6 %collective-permute-start = (bf16[64,1024]{1,0:T(8,128)(2,1)}, bf16[64,1024]{1,0:T(8,128)(2,1)S(1)}, u32[]{:S(2)}, u32[]{:S(2)}) collective-permute-start(bf16[64,1024]{1,0:T(8,128)(2,1)} %source.1), channel_id=1, source_target_pairs={{0,1},{1,0},{2,3},{3,2},{4,5},{5,4},{6,7},{7,6},{8,9},{9,8},{10,11... | collective-permute-start | bytes 393224 | tf_op jit(solution)/shard_map/ppermute | solution.py:44
  1.6 0.9 %copy-done.1 = bf16[64,1024]{1,0:T(8,128)(2,1)S(1)} copy-done((bf16[64,1024]{1,0:T(8,128)(2,1)S(1)}, bf16[64,1024]{1,0:T(8,128)(2,1)}, u32[]{:S(2)}) %copy-start.1) | copy-done | bytes 131096
  2.7 1.4 %select_reduce_fusion = f32[1024]{0:T(1024)S(1)} fusion(f32[1024]{0:T(1024)} %param.13, s32[1024]{0:T(1024)} %param.14), kind=kLoop, calls=%fused_computation | loop fusion | flops 3144704 | bytes 12288 | tf_op jit(solution)/shard_map/reduce_sum | solution.py:295
  4.0 0.8 %fusion.7 = (f32[2]{0:T(128)S(1)}, f32[2]{0:T(128)S(1)}) fusion(f32[64]{0:T(128)} %param.12, s32[]{:T(128)S(6)} %select_n.74, s32[]{:T(128)S(6)} %select_n.72), kind=kLoop, calls=%fused_computation.21 | loop fusion | bytes 40 | tf_op jit(solution)/shard_map/dynamic_slice | solution.py:299
  5.5 1.9 %collective-permute-start.2 = (bf16[128,1024]{1,0:T(8,128)(2,1)S(1)}, bf16[128,1024]{1,0:T(8,128)(2,1)S(1)}, u32[]{:S(2)}, u32[]{:S(2)}) collective-permute-start(bf16[128,1024]{1,0:T(8,128)(2,1)S(1)} %shard_map.94.first), channel_id=1, source_target_pairs={{0,2},{1,3},{2,4},{3,5},{4,6},{5,7},{6,0},{7,1},{8,10},{9,11},{10,... | collective-permute-start | bytes 786440 | tf_op jit(solution)/shard_map/ppermute | solution.py:44
  7.4 1.5 %collective-permute-start.5 = (bf16[128,1024]{1,0:T(8,128)(2,1)S(1)}, bf16[128,1024]{1,0:T(8,128)(2,1)S(1)}, u32[]{:S(2)}, u32[]{:S(2)}) collective-permute-start(bf16[128,1024]{1,0:T(8,128)(2,1)S(1)} %shard_map.94.first), channel_id=1, source_target_pairs={{0,6},{1,7},{2,0},{3,1},{4,2},{5,3},{6,4},{7,5},{8,14},{9,15},{10,... | collective-permute-start | bytes 786440 | tf_op jit(solution)/shard_map/ppermute | solution.py:44
  8.9 2.1 %collective-permute-start.6 = (bf16[128,1024]{1,0:T(8,128)(2,1)S(1)}, bf16[128,1024]{1,0:T(8,128)(2,1)S(1)}, u32[]{:S(2)}, u32[]{:S(2)}) collective-permute-start(bf16[128,1024]{1,0:T(8,128)(2,1)S(1)} %shard_map.94.first), channel_id=1, source_target_pairs={{0,4},{1,5},{2,6},{3,7},{4,0},{5,1},{6,2},{7,3},{8,12},{9,13},{10,... | collective-permute-start | bytes 786440 | tf_op jit(solution)/shard_map/ppermute | solution.py:44
  11.0 0.7 %fusion.6 = s32[32]{0:T(128)S(1)} fusion(s32[32]{0:T(128)} %constant.86.clone, s32[32]{0:T(128)} %constant.87.clone, pred[]{:T(512)S(6)} %eq.26, s32[32]{0:T(128)} %constant.88.clone, s32[]{:T(128)S(6)} %select_n.71, s32[]{:T(128)S(6)} %select_n.67, s32[]{:T(128)S(6)} %select_n.65, s32[]{:T(128)S(6)} %mul.21), kind=kLoop, calls=%fused_computation.19 | loop fusion | flops 1024 | bytes 529 | tf_op jit(solution)/shard_map/add | solution.py:291
  11.7 3.1 %collective-permute-start.11 = (bf16[256,2048]{1,0:T(8,128)(2,1)}, bf16[256,2048]{1,0:T(8,128)(2,1)S(1)}, u32[]{:S(2)}, u32[]{:S(2)}) collective-permute-start(bf16[256,2048]{1,0:T(8,128)(2,1)} %refs_2_.7), channel_id=1, source_target_pairs={{0,64},{1,65},{2,66},{3,67},{4,68},{5,69},{6,70},{7,71},{8,72},{9,... | collective-permute-start | bytes 3145736 | tf_op jit(solution)/shard_map/ppermute | solution.py:44
  14.9 0.7 %copy-done.2 = s32[1024]{0:T(1024)S(1)} copy-done((s32[1024]{0:T(1024)S(1)}, s32[1024]{0:T(1024)}, u32[]{:S(2)}) %copy-start.2) | copy-done | bytes 4120
  15.6 1.6 %shard_map.91.refs_6_.places = s32[256]{0:T(256)S(1)} custom-call(s32[33]{0:T(128)S(1)} %pad_add_fusion.origin, s32[1024]{0:T(1024)S(1)} %copy-done.2), custom_call_target="tpu_custom_call" | custom-call | flops 1000000000 | bytes 1048576 | tf_op jit(solution)/shard_map/pallas_call | solution.py:213
  17.3 2.0 %collective-permute-start.3 = (bf16[256,1024]{1,0:T(8,128)(2,1)S(1)}, bf16[256,1024]{1,0:T(8,128)(2,1)S(1)}, u32[]{:S(2)}, u32[]{:S(2)}) collective-permute-start(bf16[256,1024]{1,0:T(8,128)(2,1)S(1)} %shard_map.95.refs_0_), channel_id=1, source_target_pairs={{0,8},{1,9},{2,10},{3,11},{4,12},{5,13},{6,14},{7,15},{8,16},{9,17... | collective-permute-start | bytes 1572872 | tf_op jit(solution)/shard_map/ppermute | solution.py:44
  19.3 2.3 %collective-permute-start.7 = (bf16[256,1024]{1,0:T(8,128)(2,1)S(1)}, bf16[256,1024]{1,0:T(8,128)(2,1)S(1)}, u32[]{:S(2)}, u32[]{:S(2)}) collective-permute-start(bf16[256,1024]{1,0:T(8,128)(2,1)S(1)} %shard_map.96.refs_1_), channel_id=1, source_target_pairs={{0,24},{1,25},{2,26},{3,27},{4,28},{5,29},{6,30},{7,31},{8,0},{9,1... | collective-permute-start | bytes 1572872 | tf_op jit(solution)/shard_map/ppermute | solution.py:44
  21.6 1.1 %shard_map.92.refs_6_.row_part = f32[2048,128]{1,0:T(8,128)S(1)} custom-call(s32[33]{0:T(128)S(1)} %pad_add_fusion.origin, s32[1024]{0:T(1024)S(1)} %copy-done.2, f32[2048,128]{1,0:T(8,128)S(1)} %broadcast_in_dim.30.row_term), custom_call_target="tpu_custom_call" | custom-call | flops 3000000000 | bytes 2097152 | tf_op jit(solution)/shard_map/pallas_call | solution.py:202
  22.7 3.2 %collective-permute-start.10 = (bf16[256,1024]{1,0:T(8,128)(2,1)S(1)}, bf16[256,1024]{1,0:T(8,128)(2,1)S(1)}, u32[]{:S(2)}, u32[]{:S(2)}) collective-permute-start(bf16[256,1024]{1,0:T(8,128)(2,1)S(1)} %shard_map.95.refs_0_), channel_id=1, source_target_pairs={{0,24},{1,25},{2,26},{3,27},{4,28},{5,29},{6,30},{7,31},{8,0},{9,1... | collective-permute-start | bytes 1572872 | tf_op jit(solution)/shard_map/ppermute | solution.py:44
  25.9 2.2 %shard_map.97 = (bf16[2048,1024]{1,0:T(8,128)(2,1)S(1)}, f32[2048,2048]{1,0:T(8,128)S(1)}) custom-call(s32[33]{0:T(128)S(1)} %pad_add_fusion.origin, bf16[256,1024]{1,0:T(8,128)(2,1)S(1)} %shard_map.95.refs_0_, bf16[256,1024]{1,0:T(8,128)(2,1)S(1)} %shard_map.96.refs_1_, bf16[256,2048]{1,0:T(8,128)(2,1)S(1)} %copy-done, ...), custom_call_target="tpu_custom_call" | custom-call | flops 3000000000 | bytes 2097152 | tf_op jit(solution)/shard_map/pallas_call | solution.py:242
  28.6 3.4 %collective-permute-start.8 = (bf16[256,1024]{1,0:T(8,128)(2,1)S(1)}, bf16[256,1024]{1,0:T(8,128)(2,1)S(1)}, u32[]{:S(2)}, u32[]{:S(2)}) collective-permute-start(bf16[256,1024]{1,0:T(8,128)(2,1)S(1)} %collective-permute-done.7.refs_1_), channel_id=1, source_target_pairs={{0,24},{1,25},{2,26},{3,27},{4,28},{5,29},{6,30},{7,31},{8,0},{9,1... | collective-permute-start | bytes 1572872 | tf_op jit(solution)/shard_map/ppermute | solution.py:44
  32.0 2.2 %shard_map.98 = (bf16[2048,1024]{1,0:T(8,128)(2,1)S(1)}, f32[2048,2048]{1,0:T(8,128)S(1)}) custom-call(s32[33]{0:T(128)S(1)} %pad_add_fusion.origin, bf16[256,1024]{1,0:T(8,128)(2,1)S(1)} %collective-permute-done.3.refs_0_, bf16[256,1024]{1,0:T(8,128)(2,1)S(1)} %collective-permute-done.7.refs_1_, ...), custom_call_target="tpu_custom_call", output_to_operand_aliasing={{0}: (5, {}), {1}: (6, {})} | custom-call | flops 3000000000 | bytes 2097152 | tf_op jit(solution)/shard_map/pallas_call | solution.py:242
  34.2 2.2 %shard_map.99 = (bf16[2048,1024]{1,0:T(8,128)(2,1)S(1)}, f32[2048,2048]{1,0:T(8,128)S(1)}) custom-call(s32[33]{0:T(128)S(1)} %pad_add_fusion.origin, bf16[256,1024]{1,0:T(8,128)(2,1)S(1)} %collective-permute-done.9.refs_0_, bf16[256,1024]{1,0:T(8,128)(2,1)S(1)} %collective-permute-done.10.refs_1_, ...), custom_call_target="tpu_custom_call", output_to_operand_aliasing={{0}: (5, {}), {1}: (6, {})} | custom-call | flops 1000000000 | bytes 2097152 | tf_op jit(solution)/shard_map/pallas_call | solution.py:242
  36.4 2.3 %collective-permute-done.11.across = bf16[256,2048]{1,0:T(8,128)(2,1)S(1)} collective-permute-done((bf16[256,2048]{1,0:T(8,128)(2,1)}, bf16[256,2048]{1,0:T(8,128)(2,1)S(1)}, u32[]{:S(2)}, u32[]{:S(2)}) %collective-permute-start.11) | collective-permute-done | bytes 1048608 | tf_op jit(solution)/shard_map/ppermute | solution.py:44
  38.8 1.0 %collective-permute-done.8.refs_1_ = bf16[256,1024]{1,0:T(8,128)(2,1)S(1)} collective-permute-done((bf16[256,1024]{1,0:T(8,128)(2,1)S(1)}, bf16[256,1024]{1,0:T(8,128)(2,1)S(1)}, u32[]{:S(2)}, u32[]{:S(2)}) %collective-permute-start.8) | collective-permute-done | bytes 524320 | tf_op jit(solution)/shard_map/ppermute | solution.py:44
  39.8 2.6 %collective-permute-done.4.refs_0_ = bf16[256,1024]{1,0:T(8,128)(2,1)S(1)} collective-permute-done((bf16[256,1024]{1,0:T(8,128)(2,1)S(1)}, bf16[256,1024]{1,0:T(8,128)(2,1)S(1)}, u32[]{:S(2)}, u32[]{:S(2)}) %collective-permute-start.4) | collective-permute-done | bytes 524320 | tf_op jit(solution)/shard_map/ppermute | solution.py:44
  42.4 2.2 %shard_map.101 = (bf16[2048,1024]{1,0:T(8,128)(2,1)S(1)}, f32[2048,2048]{1,0:T(8,128)S(1)}) custom-call(s32[33]{0:T(128)S(1)} %pad_add_fusion.origin, bf16[256,1024]{1,0:T(8,128)(2,1)S(1)} %collective-permute-done.4.refs_0_, bf16[256,1024]{1,0:T(8,128)(2,1)S(1)} %collective-permute-done.8.refs_1_, ...), custom_call_target="tpu_custom_call", output_to_operand_aliasing={{0}: (5, {}), {1}: (6, {})} | custom-call | flops 12000000000 | bytes 2097152 | tf_op jit(solution)/shard_map/pallas_call | solution.py:242
  44.6 9.3 %shard_map.102 = f32[2048,2048]{1,0:T(8,128)} custom-call(s32[33]{0:T(128)S(1)} %pad_add_fusion.origin, s32[256]{0:T(256)S(1)} %shard_map.91.refs_6_.places, f32[2048,128]{1,0:T(8,128)S(1)} %shard_map.92.refs_6_.row_part, f32[1,2048]{1,0:T(1,128)S(1)} %bitcast.10, bf16[2048,1024]{1,0:T(8,128)(2,1)S(1)} %get-tuple-element.32.held, ...), custom_call_target="tpu_custom_call" | custom-call | flops 1 | bytes 8388608 | tf_op jit(solution)/shard_map/pallas_call | solution.py:257
  (28 shorter events, 1.3 us)
Async XLA Ops:
  0.0 5.3 %collective-permute-start = (bf16[64,1024]{1,0:T(8,128)(2,1)}, bf16[64,1024]{1,0:T(8,128)(2,1)S(1)}, u32[]{:S(2)}, u32[]{:S(2)}) collective-permute-start(bf16[64,1024]{1,0:T(8,128)(2,1)} %source.1), channel_id=1, source_target_pairs={{0,1},{1,0},{2,3},{3,2},{4,5},{5,4},{6,7},{7,6},{8,9},{9,8},{10,11... | collective-permute-start | bytes 393224 | tf_op jit(solution)/shard_map/ppermute | solution.py:44
  1.6 0.9 %copy-start.1 = (bf16[64,1024]{1,0:T(8,128)(2,1)S(1)}, bf16[64,1024]{1,0:T(8,128)(2,1)}, u32[]{:S(2)}) copy-start(bf16[64,1024]{1,0:T(8,128)(2,1)} %source.1) | copy-start | bytes 393220
  5.3 11.9 %collective-permute-start.1 = (bf16[256,2048]{1,0:T(8,128)(2,1)}, bf16[256,2048]{1,0:T(8,128)(2,1)S(1)}, u32[]{:S(2)}, u32[]{:S(2)}) collective-permute-start(bf16[256,2048]{1,0:T(8,128)(2,1)} %refs_2_.7), channel_id=1, source_target_pairs={{0,32},{1,33},{2,34},{3,35},{4,36},{5,37},{6,38},{7,39},{8,40},{9,... | collective-permute-start | bytes 3145736 | tf_op jit(solution)/shard_map/ppermute | solution.py:44
  5.5 11.8 %collective-permute-start.2 = (bf16[128,1024]{1,0:T(8,128)(2,1)S(1)}, bf16[128,1024]{1,0:T(8,128)(2,1)S(1)}, u32[]{:S(2)}, u32[]{:S(2)}) collective-permute-start(bf16[128,1024]{1,0:T(8,128)(2,1)S(1)} %shard_map.94.first), channel_id=1, source_target_pairs={{0,2},{1,3},{2,4},{3,5},{4,6},{5,7},{6,0},{7,1},{8,10},{9,11},{10,... | collective-permute-start | bytes 786440 | tf_op jit(solution)/shard_map/ppermute | solution.py:44
  7.4 11.9 %collective-permute-start.5 = (bf16[128,1024]{1,0:T(8,128)(2,1)S(1)}, bf16[128,1024]{1,0:T(8,128)(2,1)S(1)}, u32[]{:S(2)}, u32[]{:S(2)}) collective-permute-start(bf16[128,1024]{1,0:T(8,128)(2,1)S(1)} %shard_map.94.first), channel_id=1, source_target_pairs={{0,6},{1,7},{2,0},{3,1},{4,2},{5,3},{6,4},{7,5},{8,14},{9,15},{10,... | collective-permute-start | bytes 786440 | tf_op jit(solution)/shard_map/ppermute | solution.py:44
  8.9 10.4 %collective-permute-start.6 = (bf16[128,1024]{1,0:T(8,128)(2,1)S(1)}, bf16[128,1024]{1,0:T(8,128)(2,1)S(1)}, u32[]{:S(2)}, u32[]{:S(2)}) collective-permute-start(bf16[128,1024]{1,0:T(8,128)(2,1)S(1)} %shard_map.94.first), channel_id=1, source_target_pairs={{0,4},{1,5},{2,6},{3,7},{4,0},{5,1},{6,2},{7,3},{8,12},{9,13},{10,... | collective-permute-start | bytes 786440 | tf_op jit(solution)/shard_map/ppermute | solution.py:44
  11.7 27.1 %collective-permute-start.11 = (bf16[256,2048]{1,0:T(8,128)(2,1)}, bf16[256,2048]{1,0:T(8,128)(2,1)S(1)}, u32[]{:S(2)}, u32[]{:S(2)}) collective-permute-start(bf16[256,2048]{1,0:T(8,128)(2,1)} %refs_2_.7), channel_id=1, source_target_pairs={{0,64},{1,65},{2,66},{3,67},{4,68},{5,69},{6,70},{7,71},{8,72},{9,... | collective-permute-start | bytes 3145736 | tf_op jit(solution)/shard_map/ppermute | solution.py:44
  14.9 0.7 %copy-start.2 = (s32[1024]{0:T(1024)S(1)}, s32[1024]{0:T(1024)}, u32[]{:S(2)}) copy-start(s32[1024]{0:T(1024)} %block_place.3) | copy-start | bytes 12292
  17.3 14.7 %collective-permute-start.3 = (bf16[256,1024]{1,0:T(8,128)(2,1)S(1)}, bf16[256,1024]{1,0:T(8,128)(2,1)S(1)}, u32[]{:S(2)}, u32[]{:S(2)}) collective-permute-start(bf16[256,1024]{1,0:T(8,128)(2,1)S(1)} %shard_map.95.refs_0_), channel_id=1, source_target_pairs={{0,8},{1,9},{2,10},{3,11},{4,12},{5,13},{6,14},{7,15},{8,16},{9,17... | collective-permute-start | bytes 1572872 | tf_op jit(solution)/shard_map/ppermute | solution.py:44
  19.3 6.6 %copy-start = (bf16[256,2048]{1,0:T(8,128)(2,1)S(1)}, bf16[256,2048]{1,0:T(8,128)(2,1)}, u32[]{:S(2)}) copy-start(bf16[256,2048]{1,0:T(8,128)(2,1)} %refs_2_.7) | copy-start | bytes 3145732
  19.3 9.3 %collective-permute-start.7 = (bf16[256,1024]{1,0:T(8,128)(2,1)S(1)}, bf16[256,1024]{1,0:T(8,128)(2,1)S(1)}, u32[]{:S(2)}, u32[]{:S(2)}) collective-permute-start(bf16[256,1024]{1,0:T(8,128)(2,1)S(1)} %shard_map.96.refs_1_), channel_id=1, source_target_pairs={{0,24},{1,25},{2,26},{3,27},{4,28},{5,29},{6,30},{7,31},{8,0},{9,1... | collective-permute-start | bytes 1572872 | tf_op jit(solution)/shard_map/ppermute | solution.py:44
  22.6 11.6 %collective-permute-start.9 = (bf16[256,1024]{1,0:T(8,128)(2,1)S(1)}, bf16[256,1024]{1,0:T(8,128)(2,1)S(1)}, u32[]{:S(2)}, u32[]{:S(2)}) collective-permute-start(bf16[256,1024]{1,0:T(8,128)(2,1)S(1)} %shard_map.96.refs_1_), channel_id=1, source_target_pairs={{0,8},{1,9},{2,10},{3,11},{4,12},{5,13},{6,14},{7,15},{8,16},{9,17... | collective-permute-start | bytes 1572872 | tf_op jit(solution)/shard_map/ppermute | solution.py:44
  22.7 11.5 %collective-permute-start.10 = (bf16[256,1024]{1,0:T(8,128)(2,1)S(1)}, bf16[256,1024]{1,0:T(8,128)(2,1)S(1)}, u32[]{:S(2)}, u32[]{:S(2)}) collective-permute-start(bf16[256,1024]{1,0:T(8,128)(2,1)S(1)} %shard_map.95.refs_0_), channel_id=1, source_target_pairs={{0,24},{1,25},{2,26},{3,27},{4,28},{5,29},{6,30},{7,31},{8,0},{9,1... | collective-permute-start | bytes 1572872 | tf_op jit(solution)/shard_map/ppermute | solution.py:44
  28.6 11.2 %collective-permute-start.8 = (bf16[256,1024]{1,0:T(8,128)(2,1)S(1)}, bf16[256,1024]{1,0:T(8,128)(2,1)S(1)}, u32[]{:S(2)}, u32[]{:S(2)}) collective-permute-start(bf16[256,1024]{1,0:T(8,128)(2,1)S(1)} %collective-permute-done.7.refs_1_), channel_id=1, source_target_pairs={{0,24},{1,25},{2,26},{3,27},{4,28},{5,29},{6,30},{7,31},{8,0},{9,1... | collective-permute-start | bytes 1572872 | tf_op jit(solution)/shard_map/ppermute | solution.py:44
  32.0 10.4 %collective-permute-start.4 = (bf16[256,1024]{1,0:T(8,128)(2,1)S(1)}, bf16[256,1024]{1,0:T(8,128)(2,1)S(1)}, u32[]{:S(2)}, u32[]{:S(2)}) collective-permute-start(bf16[256,1024]{1,0:T(8,128)(2,1)S(1)} %collective-permute-done.3.refs_0_), channel_id=1, source_target_pairs={{0,8},{1,9},{2,10},{3,11},{4,12},{5,13},{6,14},{7,15},{8,16},{9,17... | collective-permute-start | bytes 1572872 | tf_op jit(solution)/shard_map/ppermute | solution.py:44
  38.8 5.8 %collective-permute-start.12 = (bf16[256,2048]{1,0:T(8,128)(2,1)S(1)}, bf16[256,2048]{1,0:T(8,128)(2,1)S(1)}, u32[]{:S(2)}, u32[]{:S(2)}) collective-permute-start(bf16[256,2048]{1,0:T(8,128)(2,1)S(1)} %collective-permute-done.11.across), channel_id=1, source_target_pairs={{0,32},{1,33},{2,34},{3,35},{4,36},{5,37},{6,38},{7,39},{8,40},{9,... | collective-permute-start | bytes 3145736 | tf_op jit(solution)/shard_map/ppermute | solution.py:44

commit v5 on v4

--- a/solution.py
+++ b/solution.py
@@ -135,7 +135,7 @@
         sums[rows, at] = total
         return carry
 
-    lax.fori_loop(0, sums.shape[1] // TILE, tile, 0, unroll=4)
+    lax.fori_loop(0, sums.shape[1] // TILE, tile, 0, unroll=8)
 
 
 def finish(origin, places, row_part, col_term, held, sums, across, aslant, out, stage, sem):

time: 54.5 us -> 54.2 us (level)
  Pallas kernels: 21.1 us -> 19.7 us
  waiting for transfers between devices: 6.36 us -> 7.37 us
    pallas_call x4, Pallas kernels: 8.86 us -> 7.52 us  [begun(): pl.pallas_call(functools.partial(begin, pair), out_shape=shapes, in_specs...]
    ppermute x13, waiting for transfers between devices: 6.36 us -> 7.37 us  [send(): return lax.ppermute(value, ('row', 'col'), pairs)]
  transfers between devices with their start and end apart: 13 -> 13, of which waited for: 4 -> 5; matrix products, arithmetic and copies ran while one was open for 6% -> 6% of each run, Pallas kernels for 22% -> 19%
where the time goes in v5:
time: 54.2 us; the launch traced here: 53.5 us
  starting transfers between devices  21.2 us (39%)
  Pallas kernels  19.7 us (36%)
  waiting for transfers between devices  7.37 us (14%)
  local copies, waits for them, and re-layouts  2.78 us (5%)
  other arithmetic  2.21 us (4%)
    ppermute x13, starting transfers between devices, send(): return lax.ppermute(value, ('row', 'col'), pairs)  21.2 us
    pallas_call x1, Pallas kernels, finished(): pl.pallas_call(finish, out_shape=jax.ShapeDtypeStruct(shape, jnp.float32)...  9.28 us
    pallas_call x4, Pallas kernels, begun(): pl.pallas_call(functools.partial(begin, pair), out_shape=shapes, in_specs...  7.52 us
    ppermute x13, waiting for transfers between devices, send(): return lax.ppermute(value, ('row', 'col'), pairs)  7.37 us
    unnamed x8, local copies, waits for them, and re-layouts  1.64 us
    pallas_call x1, Pallas kernels, listed(): pl.pallas_call(list_places, out_shape=jax.ShapeDtypeStruct((256,), jnp.in...  1.63 us
    reduce_sum x1, other arithmetic, per_device(): jnp.sum(jnp.where(vir_order[:, None] == indices[None, :], vir_energy[None...  1.36 us
  transfers between devices with their start and end apart: 13, of which 5 were waited for; matrix products, arithmetic and copies ran while one was open for 6% of the time, Pallas kernels for 19%

profile of v5, /device:TPU:0, one launch (start us, length us, event | category | flops | bytes accessed | tf_op | source)
XLA Modules:
  0.0 53.5 jit_solution(15079648093627902281)
XLA Ops:
  0.0 1.6 %collective-permute-start = (bf16[64,1024]{1,0:T(8,128)(2,1)}, bf16[64,1024]{1,0:T(8,128)(2,1)S(1)}, u32[]{:S(2)}, u32[]{:S(2)}) collective-permute-start(bf16[64,1024]{1,0:T(8,128)(2,1)} %source.1), channel_id=1, source_target_pairs={{0,1},{1,0},{2,3},{3,2},{4,5},{5,4},{6,7},{7,6},{8,9},{9,8},{10,11... | collective-permute-start | bytes 393224 | tf_op jit(solution)/shard_map/ppermute | solution.py:44
  1.6 0.9 %copy-done.1 = bf16[64,1024]{1,0:T(8,128)(2,1)S(1)} copy-done((bf16[64,1024]{1,0:T(8,128)(2,1)S(1)}, bf16[64,1024]{1,0:T(8,128)(2,1)}, u32[]{:S(2)}) %copy-start.1) | copy-done | bytes 131096
  2.7 1.4 %select_reduce_fusion = f32[1024]{0:T(1024)S(1)} fusion(f32[1024]{0:T(1024)} %param.13, s32[1024]{0:T(1024)} %param.14), kind=kLoop, calls=%fused_computation | loop fusion | flops 3144704 | bytes 12288 | tf_op jit(solution)/shard_map/reduce_sum | solution.py:295
  4.0 0.8 %fusion.7 = (f32[2]{0:T(128)S(1)}, f32[2]{0:T(128)S(1)}) fusion(f32[64]{0:T(128)} %param.12, s32[]{:T(128)S(6)} %select_n.74, s32[]{:T(128)S(6)} %select_n.72), kind=kLoop, calls=%fused_computation.21 | loop fusion | bytes 40 | tf_op jit(solution)/shard_map/dynamic_slice | solution.py:299
  5.5 1.9 %collective-permute-start.2 = (bf16[128,1024]{1,0:T(8,128)(2,1)S(1)}, bf16[128,1024]{1,0:T(8,128)(2,1)S(1)}, u32[]{:S(2)}, u32[]{:S(2)}) collective-permute-start(bf16[128,1024]{1,0:T(8,128)(2,1)S(1)} %shard_map.94.first), channel_id=1, source_target_pairs={{0,2},{1,3},{2,4},{3,5},{4,6},{5,7},{6,0},{7,1},{8,10},{9,11},{10,... | collective-permute-start | bytes 786440 | tf_op jit(solution)/shard_map/ppermute | solution.py:44
  7.4 1.5 %collective-permute-start.5 = (bf16[128,1024]{1,0:T(8,128)(2,1)S(1)}, bf16[128,1024]{1,0:T(8,128)(2,1)S(1)}, u32[]{:S(2)}, u32[]{:S(2)}) collective-permute-start(bf16[128,1024]{1,0:T(8,128)(2,1)S(1)} %shard_map.94.first), channel_id=1, source_target_pairs={{0,6},{1,7},{2,0},{3,1},{4,2},{5,3},{6,4},{7,5},{8,14},{9,15},{10,... | collective-permute-start | bytes 786440 | tf_op jit(solution)/shard_map/ppermute | solution.py:44
  8.9 2.1 %collective-permute-start.6 = (bf16[128,1024]{1,0:T(8,128)(2,1)S(1)}, bf16[128,1024]{1,0:T(8,128)(2,1)S(1)}, u32[]{:S(2)}, u32[]{:S(2)}) collective-permute-start(bf16[128,1024]{1,0:T(8,128)(2,1)S(1)} %shard_map.94.first), channel_id=1, source_target_pairs={{0,4},{1,5},{2,6},{3,7},{4,0},{5,1},{6,2},{7,3},{8,12},{9,13},{10,... | collective-permute-start | bytes 786440 | tf_op jit(solution)/shard_map/ppermute | solution.py:44
  11.0 0.7 %fusion.6 = s32[32]{0:T(128)S(1)} fusion(s32[32]{0:T(128)} %constant.86.clone, s32[32]{0:T(128)} %constant.87.clone, pred[]{:T(512)S(6)} %eq.26, s32[32]{0:T(128)} %constant.88.clone, s32[]{:T(128)S(6)} %select_n.71, s32[]{:T(128)S(6)} %select_n.67, s32[]{:T(128)S(6)} %select_n.65, s32[]{:T(128)S(6)} %mul.21), kind=kLoop, calls=%fused_computation.19 | loop fusion | flops 1024 | bytes 529 | tf_op jit(solution)/shard_map/add | solution.py:291
  11.7 3.1 %collective-permute-start.11 = (bf16[256,2048]{1,0:T(8,128)(2,1)}, bf16[256,2048]{1,0:T(8,128)(2,1)S(1)}, u32[]{:S(2)}, u32[]{:S(2)}) collective-permute-start(bf16[256,2048]{1,0:T(8,128)(2,1)} %refs_2_.7), channel_id=1, source_target_pairs={{0,64},{1,65},{2,66},{3,67},{4,68},{5,69},{6,70},{7,71},{8,72},{9,... | collective-permute-start | bytes 3145736 | tf_op jit(solution)/shard_map/ppermute | solution.py:44
  15.6 1.6 %shard_map.91.refs_6_.places = s32[256]{0:T(256)S(1)} custom-call(s32[33]{0:T(128)S(1)} %pad_add_fusion.origin, s32[1024]{0:T(1024)S(1)} %copy-done.2), custom_call_target="tpu_custom_call" | custom-call | flops 1000000000 | bytes 1048576 | tf_op jit(solution)/shard_map/pallas_call | solution.py:213
  17.3 2.0 %collective-permute-start.3 = (bf16[256,1024]{1,0:T(8,128)(2,1)S(1)}, bf16[256,1024]{1,0:T(8,128)(2,1)S(1)}, u32[]{:S(2)}, u32[]{:S(2)}) collective-permute-start(bf16[256,1024]{1,0:T(8,128)(2,1)S(1)} %shard_map.95.refs_0_), channel_id=1, source_target_pairs={{0,8},{1,9},{2,10},{3,11},{4,12},{5,13},{6,14},{7,15},{8,16},{9,17... | collective-permute-start | bytes 1572872 | tf_op jit(solution)/shard_map/ppermute | solution.py:44
  19.3 2.3 %collective-permute-start.7 = (bf16[256,1024]{1,0:T(8,128)(2,1)S(1)}, bf16[256,1024]{1,0:T(8,128)(2,1)S(1)}, u32[]{:S(2)}, u32[]{:S(2)}) collective-permute-start(bf16[256,1024]{1,0:T(8,128)(2,1)S(1)} %shard_map.96.refs_1_), channel_id=1, source_target_pairs={{0,24},{1,25},{2,26},{3,27},{4,28},{5,29},{6,30},{7,31},{8,0},{9,1... | collective-permute-start | bytes 1572872 | tf_op jit(solution)/shard_map/ppermute | solution.py:44
  21.6 1.1 %shard_map.92.refs_6_.row_part = f32[2048,128]{1,0:T(8,128)S(1)} custom-call(s32[33]{0:T(128)S(1)} %pad_add_fusion.origin, s32[1024]{0:T(1024)S(1)} %copy-done.2, f32[2048,128]{1,0:T(8,128)S(1)} %broadcast_in_dim.30.row_term), custom_call_target="tpu_custom_call" | custom-call | flops 3000000000 | bytes 2097152 | tf_op jit(solution)/shard_map/pallas_call | solution.py:202
  22.7 3.2 %collective-permute-start.10 = (bf16[256,1024]{1,0:T(8,128)(2,1)S(1)}, bf16[256,1024]{1,0:T(8,128)(2,1)S(1)}, u32[]{:S(2)}, u32[]{:S(2)}) collective-permute-start(bf16[256,1024]{1,0:T(8,128)(2,1)S(1)} %shard_map.95.refs_0_), channel_id=1, source_target_pairs={{0,24},{1,25},{2,26},{3,27},{4,28},{5,29},{6,30},{7,31},{8,0},{9,1... | collective-permute-start | bytes 1572872 | tf_op jit(solution)/shard_map/ppermute | solution.py:44
  25.9 1.9 %shard_map.97 = (bf16[2048,1024]{1,0:T(8,128)(2,1)S(1)}, f32[2048,2048]{1,0:T(8,128)S(1)}) custom-call(s32[33]{0:T(128)S(1)} %pad_add_fusion.origin, bf16[256,1024]{1,0:T(8,128)(2,1)S(1)} %shard_map.95.refs_0_, bf16[256,1024]{1,0:T(8,128)(2,1)S(1)} %shard_map.96.refs_1_, bf16[256,2048]{1,0:T(8,128)(2,1)S(1)} %copy-done, ...), custom_call_target="tpu_custom_call" | custom-call | flops 3000000000 | bytes 2097152 | tf_op jit(solution)/shard_map/pallas_call | solution.py:242
  27.8 0.7 %collective-permute-done.7.refs_1_ = bf16[256,1024]{1,0:T(8,128)(2,1)S(1)} collective-permute-done((bf16[256,1024]{1,0:T(8,128)(2,1)S(1)}, bf16[256,1024]{1,0:T(8,128)(2,1)S(1)}, u32[]{:S(2)}, u32[]{:S(2)}) %collective-permute-start.7) | collective-permute-done | bytes 524320 | tf_op jit(solution)/shard_map/ppermute | solution.py:44
  28.6 3.4 %collective-permute-start.8 = (bf16[256,1024]{1,0:T(8,128)(2,1)S(1)}, bf16[256,1024]{1,0:T(8,128)(2,1)S(1)}, u32[]{:S(2)}, u32[]{:S(2)}) collective-permute-start(bf16[256,1024]{1,0:T(8,128)(2,1)S(1)} %collective-permute-done.7.refs_1_), channel_id=1, source_target_pairs={{0,24},{1,25},{2,26},{3,27},{4,28},{5,29},{6,30},{7,31},{8,0},{9,1... | collective-permute-start | bytes 1572872 | tf_op jit(solution)/shard_map/ppermute | solution.py:44
  32.0 1.9 %shard_map.98 = (bf16[2048,1024]{1,0:T(8,128)(2,1)S(1)}, f32[2048,2048]{1,0:T(8,128)S(1)}) custom-call(s32[33]{0:T(128)S(1)} %pad_add_fusion.origin, bf16[256,1024]{1,0:T(8,128)(2,1)S(1)} %collective-permute-done.3.refs_0_, bf16[256,1024]{1,0:T(8,128)(2,1)S(1)} %collective-permute-done.7.refs_1_, ...), custom_call_target="tpu_custom_call", output_to_operand_aliasing={{0}: (5, {}), {1}: (6, {})} | custom-call | flops 3000000000 | bytes 2097152 | tf_op jit(solution)/shard_map/pallas_call | solution.py:242
  34.2 1.9 %shard_map.99 = (bf16[2048,1024]{1,0:T(8,128)(2,1)S(1)}, f32[2048,2048]{1,0:T(8,128)S(1)}) custom-call(s32[33]{0:T(128)S(1)} %pad_add_fusion.origin, bf16[256,1024]{1,0:T(8,128)(2,1)S(1)} %collective-permute-done.9.refs_0_, bf16[256,1024]{1,0:T(8,128)(2,1)S(1)} %collective-permute-done.10.refs_1_, ...), custom_call_target="tpu_custom_call", output_to_operand_aliasing={{0}: (5, {}), {1}: (6, {})} | custom-call | flops 1000000000 | bytes 2097152 | tf_op jit(solution)/shard_map/pallas_call | solution.py:242
  36.1 2.7 %collective-permute-done.11.across = bf16[256,2048]{1,0:T(8,128)(2,1)S(1)} collective-permute-done((bf16[256,2048]{1,0:T(8,128)(2,1)}, bf16[256,2048]{1,0:T(8,128)(2,1)S(1)}, u32[]{:S(2)}, u32[]{:S(2)}) %collective-permute-start.11) | collective-permute-done | bytes 1048608 | tf_op jit(solution)/shard_map/ppermute | solution.py:44
  38.8 1.0 %collective-permute-done.8.refs_1_ = bf16[256,1024]{1,0:T(8,128)(2,1)S(1)} collective-permute-done((bf16[256,1024]{1,0:T(8,128)(2,1)S(1)}, bf16[256,1024]{1,0:T(8,128)(2,1)S(1)}, u32[]{:S(2)}, u32[]{:S(2)}) %collective-permute-start.8) | collective-permute-done | bytes 524320 | tf_op jit(solution)/shard_map/ppermute | solution.py:44
  39.8 2.6 %collective-permute-done.4.refs_0_ = bf16[256,1024]{1,0:T(8,128)(2,1)S(1)} collective-permute-done((bf16[256,1024]{1,0:T(8,128)(2,1)S(1)}, bf16[256,1024]{1,0:T(8,128)(2,1)S(1)}, u32[]{:S(2)}, u32[]{:S(2)}) %collective-permute-start.4) | collective-permute-done | bytes 524320 | tf_op jit(solution)/shard_map/ppermute | solution.py:44
  42.4 1.9 %shard_map.101 = (bf16[2048,1024]{1,0:T(8,128)(2,1)S(1)}, f32[2048,2048]{1,0:T(8,128)S(1)}) custom-call(s32[33]{0:T(128)S(1)} %pad_add_fusion.origin, bf16[256,1024]{1,0:T(8,128)(2,1)S(1)} %collective-permute-done.4.refs_0_, bf16[256,1024]{1,0:T(8,128)(2,1)S(1)} %collective-permute-done.8.refs_1_, ...), custom_call_target="tpu_custom_call", output_to_operand_aliasing={{0}: (5, {}), {1}: (6, {})} | custom-call | flops 12000000000 | bytes 2097152 | tf_op jit(solution)/shard_map/pallas_call | solution.py:242
  44.2 9.3 %shard_map.102 = f32[2048,2048]{1,0:T(8,128)} custom-call(s32[33]{0:T(128)S(1)} %pad_add_fusion.origin, s32[256]{0:T(256)S(1)} %shard_map.91.refs_6_.places, f32[2048,128]{1,0:T(8,128)S(1)} %shard_map.92.refs_6_.row_part, f32[1,2048]{1,0:T(1,128)S(1)} %bitcast.10, bf16[2048,1024]{1,0:T(8,128)(2,1)S(1)} %get-tuple-element.32.held, ...), custom_call_target="tpu_custom_call" | custom-call | flops 1 | bytes 8388608 | tf_op jit(solution)/shard_map/pallas_call | solution.py:257
  (28 shorter events, 1.9 us)
Async XLA Ops:
  0.0 5.3 %collective-permute-start = (bf16[64,1024]{1,0:T(8,128)(2,1)}, bf16[64,1024]{1,0:T(8,128)(2,1)S(1)}, u32[]{:S(2)}, u32[]{:S(2)}) collective-permute-start(bf16[64,1024]{1,0:T(8,128)(2,1)} %source.1), channel_id=1, source_target_pairs={{0,1},{1,0},{2,3},{3,2},{4,5},{5,4},{6,7},{7,6},{8,9},{9,8},{10,11... | collective-permute-start | bytes 393224 | tf_op jit(solution)/shard_map/ppermute | solution.py:44
  1.6 0.9 %copy-start.1 = (bf16[64,1024]{1,0:T(8,128)(2,1)S(1)}, bf16[64,1024]{1,0:T(8,128)(2,1)}, u32[]{:S(2)}) copy-start(bf16[64,1024]{1,0:T(8,128)(2,1)} %source.1) | copy-start | bytes 393220
  5.3 11.9 %collective-permute-start.1 = (bf16[256,2048]{1,0:T(8,128)(2,1)}, bf16[256,2048]{1,0:T(8,128)(2,1)S(1)}, u32[]{:S(2)}, u32[]{:S(2)}) collective-permute-start(bf16[256,2048]{1,0:T(8,128)(2,1)} %refs_2_.7), channel_id=1, source_target_pairs={{0,32},{1,33},{2,34},{3,35},{4,36},{5,37},{6,38},{7,39},{8,40},{9,... | collective-permute-start | bytes 3145736 | tf_op jit(solution)/shard_map/ppermute | solution.py:44
  5.5 11.8 %collective-permute-start.2 = (bf16[128,1024]{1,0:T(8,128)(2,1)S(1)}, bf16[128,1024]{1,0:T(8,128)(2,1)S(1)}, u32[]{:S(2)}, u32[]{:S(2)}) collective-permute-start(bf16[128,1024]{1,0:T(8,128)(2,1)S(1)} %shard_map.94.first), channel_id=1, source_target_pairs={{0,2},{1,3},{2,4},{3,5},{4,6},{5,7},{6,0},{7,1},{8,10},{9,11},{10,... | collective-permute-start | bytes 786440 | tf_op jit(solution)/shard_map/ppermute | solution.py:44
  7.4 11.9 %collective-permute-start.5 = (bf16[128,1024]{1,0:T(8,128)(2,1)S(1)}, bf16[128,1024]{1,0:T(8,128)(2,1)S(1)}, u32[]{:S(2)}, u32[]{:S(2)}) collective-permute-start(bf16[128,1024]{1,0:T(8,128)(2,1)S(1)} %shard_map.94.first), channel_id=1, source_target_pairs={{0,6},{1,7},{2,0},{3,1},{4,2},{5,3},{6,4},{7,5},{8,14},{9,15},{10,... | collective-permute-start | bytes 786440 | tf_op jit(solution)/shard_map/ppermute | solution.py:44
  8.9 10.4 %collective-permute-start.6 = (bf16[128,1024]{1,0:T(8,128)(2,1)S(1)}, bf16[128,1024]{1,0:T(8,128)(2,1)S(1)}, u32[]{:S(2)}, u32[]{:S(2)}) collective-permute-start(bf16[128,1024]{1,0:T(8,128)(2,1)S(1)} %shard_map.94.first), channel_id=1, source_target_pairs={{0,4},{1,5},{2,6},{3,7},{4,0},{5,1},{6,2},{7,3},{8,12},{9,13},{10,... | collective-permute-start | bytes 786440 | tf_op jit(solution)/shard_map/ppermute | solution.py:44
  11.7 27.1 %collective-permute-start.11 = (bf16[256,2048]{1,0:T(8,128)(2,1)}, bf16[256,2048]{1,0:T(8,128)(2,1)S(1)}, u32[]{:S(2)}, u32[]{:S(2)}) collective-permute-start(bf16[256,2048]{1,0:T(8,128)(2,1)} %refs_2_.7), channel_id=1, source_target_pairs={{0,64},{1,65},{2,66},{3,67},{4,68},{5,69},{6,70},{7,71},{8,72},{9,... | collective-permute-start | bytes 3145736 | tf_op jit(solution)/shard_map/ppermute | solution.py:44
  14.9 0.7 %copy-start.2 = (s32[1024]{0:T(1024)S(1)}, s32[1024]{0:T(1024)}, u32[]{:S(2)}) copy-start(s32[1024]{0:T(1024)} %block_place.3) | copy-start | bytes 12292
  17.3 14.7 %collective-permute-start.3 = (bf16[256,1024]{1,0:T(8,128)(2,1)S(1)}, bf16[256,1024]{1,0:T(8,128)(2,1)S(1)}, u32[]{:S(2)}, u32[]{:S(2)}) collective-permute-start(bf16[256,1024]{1,0:T(8,128)(2,1)S(1)} %shard_map.95.refs_0_), channel_id=1, source_target_pairs={{0,8},{1,9},{2,10},{3,11},{4,12},{5,13},{6,14},{7,15},{8,16},{9,17... | collective-permute-start | bytes 1572872 | tf_op jit(solution)/shard_map/ppermute | solution.py:44
  19.3 6.6 %copy-start = (bf16[256,2048]{1,0:T(8,128)(2,1)S(1)}, bf16[256,2048]{1,0:T(8,128)(2,1)}, u32[]{:S(2)}) copy-start(bf16[256,2048]{1,0:T(8,128)(2,1)} %refs_2_.7) | copy-start | bytes 3145732
  19.3 9.3 %collective-permute-start.7 = (bf16[256,1024]{1,0:T(8,128)(2,1)S(1)}, bf16[256,1024]{1,0:T(8,128)(2,1)S(1)}, u32[]{:S(2)}, u32[]{:S(2)}) collective-permute-start(bf16[256,1024]{1,0:T(8,128)(2,1)S(1)} %shard_map.96.refs_1_), channel_id=1, source_target_pairs={{0,24},{1,25},{2,26},{3,27},{4,28},{5,29},{6,30},{7,31},{8,0},{9,1... | collective-permute-start | bytes 1572872 | tf_op jit(solution)/shard_map/ppermute | solution.py:44
  22.6 11.6 %collective-permute-start.9 = (bf16[256,1024]{1,0:T(8,128)(2,1)S(1)}, bf16[256,1024]{1,0:T(8,128)(2,1)S(1)}, u32[]{:S(2)}, u32[]{:S(2)}) collective-permute-start(bf16[256,1024]{1,0:T(8,128)(2,1)S(1)} %shard_map.96.refs_1_), channel_id=1, source_target_pairs={{0,8},{1,9},{2,10},{3,11},{4,12},{5,13},{6,14},{7,15},{8,16},{9,17... | collective-permute-start | bytes 1572872 | tf_op jit(solution)/shard_map/ppermute | solution.py:44
  22.7 11.5 %collective-permute-start.10 = (bf16[256,1024]{1,0:T(8,128)(2,1)S(1)}, bf16[256,1024]{1,0:T(8,128)(2,1)S(1)}, u32[]{:S(2)}, u32[]{:S(2)}) collective-permute-start(bf16[256,1024]{1,0:T(8,128)(2,1)S(1)} %shard_map.95.refs_0_), channel_id=1, source_target_pairs={{0,24},{1,25},{2,26},{3,27},{4,28},{5,29},{6,30},{7,31},{8,0},{9,1... | collective-permute-start | bytes 1572872 | tf_op jit(solution)/shard_map/ppermute | solution.py:44
  28.6 11.2 %collective-permute-start.8 = (bf16[256,1024]{1,0:T(8,128)(2,1)S(1)}, bf16[256,1024]{1,0:T(8,128)(2,1)S(1)}, u32[]{:S(2)}, u32[]{:S(2)}) collective-permute-start(bf16[256,1024]{1,0:T(8,128)(2,1)S(1)} %collective-permute-done.7.refs_1_), channel_id=1, source_target_pairs={{0,24},{1,25},{2,26},{3,27},{4,28},{5,29},{6,30},{7,31},{8,0},{9,1... | collective-permute-start | bytes 1572872 | tf_op jit(solution)/shard_map/ppermute | solution.py:44
  32.0 10.4 %collective-permute-start.4 = (bf16[256,1024]{1,0:T(8,128)(2,1)S(1)}, bf16[256,1024]{1,0:T(8,128)(2,1)S(1)}, u32[]{:S(2)}, u32[]{:S(2)}) collective-permute-start(bf16[256,1024]{1,0:T(8,128)(2,1)S(1)} %collective-permute-done.3.refs_0_), channel_id=1, source_target_pairs={{0,8},{1,9},{2,10},{3,11},{4,12},{5,13},{6,14},{7,15},{8,16},{9,17... | collective-permute-start | bytes 1572872 | tf_op jit(solution)/shard_map/ppermute | solution.py:44
  38.8 5.5 %collective-permute-start.12 = (bf16[256,2048]{1,0:T(8,128)(2,1)S(1)}, bf16[256,2048]{1,0:T(8,128)(2,1)S(1)}, u32[]{:S(2)}, u32[]{:S(2)}) collective-permute-start(bf16[256,2048]{1,0:T(8,128)(2,1)S(1)} %collective-permute-done.11.across), channel_id=1, source_target_pairs={{0,32},{1,33},{2,34},{3,35},{4,36},{5,37},{6,38},{7,39},{8,40},{9,... | collective-permute-start | bytes 3145736 | tf_op jit(solution)/shard_map/ppermute | solution.py:44
